TPU v7x, 128 devices: a whole 4x4x4 slice. The times are simulated.
128 devices in a mesh: gx: 16 (over y, z), gy: 4 (over x), ta: 2 (over core).
Axes of the slice: x: 4, y: 4, z: 4, core: 2. Of those that a mesh axis runs over, the one named last changes fastest.
Arguments:
- features: bfloat16 [2, 256, 256, 1280], P('ta', 'gx', 'gy'), may hold values from -6 to 6
- cotangent: bfloat16 [2, 256, 256, 1280], P('ta', 'gx', 'gy'), may hold values from -6 to 6
- spectral_weight: bfloat16 [48, 24, 2, 20, 960], P('gx', 'gy'), may hold values from -3 to 3
- mixing_weight: bfloat16 [20, 20], replicated, may hold values from -1.25 to 1.25
Outputs:
- activated: bfloat16 [2, 256, 256, 1280], P('ta', 'gx', 'gy')
- grad_features: bfloat16 [2, 256, 256, 1280], P('ta', 'gx', 'gy')
- grad_spectral: float32 [48, 24, 2, 20, 960], P('gx', ('gy', 'ta'))
- grad_mixing: float32 [20, 20], replicated
All inputs are finite; a program needn't handle non-finite values.
Results may differ from a plain program's by a relative error of at most 0.028.
Values may be sent and summed in bfloat16 or wider, within the bound.
A program may use at most 192 MiB of HBM per device.

v0:
```python
import math

import jax
import jax.numpy as jnp
import ml_dtypes
import numpy as np
from jax import lax
from jax.experimental import pallas as pl
from jax.experimental.pallas import tpu as pltpu
from jax.sharding import PartitionSpec as P

NX = 256
NY = 256
NZ = 64
C = 20
M = 24
KEPT = 48
CZ = C * NZ
GX = 16
GY = 4
ROWS = 1024
HALF = 512
F32 = jnp.float32
BF16 = jnp.bfloat16
MESH = pl.DeviceIdType.MESH
NT = (((1,), (1,)), ((), ()))
TN = (((0,), (0,)), ((), ()))


def cos_sin(length, count, folded):
    freq = np.arange(count)
    if folded:
        freq = np.where(freq < count // 2, freq, freq + length - count)
    phases = np.arange(length)[:, None] * freq[None, :] % length
    angles = phases.astype(np.float32) * np.float32(2.0 * math.pi / length)
    return np.cos(angles), np.sin(angles)


def complex_table(length, count):
    cosine, sine = cos_sin(length, count, True)
    return np.stack([np.stack([cosine, -sine], 1), np.stack([sine, cosine], 1)], 0)


def tables():
    cosine, sine = cos_sin(NZ, M, False)
    depth = np.stack([cosine, -sine], 1)
    ee = np.zeros((GY, C, NZ, 2, 128), np.float32)
    for h in range(GY):
        for jl in range(6):
            for c in range(C):
                ee[h, c, :, :, jl * C + c] = depth[:, :, h * 6 + jl]
    ee = ee.reshape(GY, CZ, 256)
    eet = np.ascontiguousarray(ee.transpose(0, 2, 1)).reshape(GY * 256, CZ)
    height = complex_table(NY, KEPT).reshape(2, GY, 64, 2, KEPT)
    a2 = np.zeros((GY, 2, 2, KEPT, 2, 2, 64), np.float32)
    for x2 in range(2):
        a2[:, x2, :, :, x2] = height.transpose(1, 3, 4, 0, 2)
    a2 = a2.reshape(GY, 192, 256)
    at2 = np.ascontiguousarray(a2.transpose(0, 2, 1))
    width = complex_table(NX, KEPT).reshape(2, GX, 2, 8, 2, KEPT)
    fx = np.zeros((2, GX, 2, 8, 2, 1024), np.float32)
    fx[..., : C * KEPT] = np.tile(width.transpose(2, 1, 0, 3, 4, 5), (1, 1, 1, 1, 1, C))
    fx = fx.reshape(512, 2048)
    pad = np.zeros((6, 24, 128), np.float32)
    for jl in range(6):
        for c in range(C):
            pad[jl, c, jl * C + c] = 1.0
    pad = pad.reshape(144, 128)
    return [t.astype(ml_dtypes.bfloat16) for t in (ee, eet, a2, at2, fx, pad)]


def kernel(
    u_hbm, cot_hbm, w_ref, mix_ref, mixt_ref, ee_hbm, eet_hbm, a2_hbm, at2_hbm, fx_hbm, pad_hbm,
    act_hbm, gf_hbm, gs_ref, gm_ref,
    u, cot, g, out, ee, eet, kron, lin, fx, pad, a2, at2, wp, uh, ut, lw, gss, gsr,
    part, dg, fl, fr, hs, hr, bs, br, ag, by, s, mask, gh, gmx, gmy, gma,
    in_sem, out_sem, rs_ss, rs_rs, h_ss, h_rs, b_ss, b_rs, ag_ss, ag_rs, gs_sem, gy_ss, gy_rs, gx_ss, gx_rs, ta_sem,
):
    me_x = lax.axis_index("gx")
    me_y = lax.axis_index("gy")
    me_t = lax.axis_index("ta")

    def at_y(rel):
        return (me_x, lax.rem(me_y + rel, GY), me_t)

    def at_x(d):
        return (lax.rem(me_x + d, GX), me_y, me_t)

    twin = (me_x, me_y, 1 - me_t)

    loads = [
        pltpu.make_async_copy(src, dst, in_sem.at[i])
        for i, (src, dst) in enumerate([
            (u_hbm, u), (ee_hbm, ee), (a2_hbm.at[me_y], a2), (fx_hbm, fx), (pad_hbm, pad),
            (at2_hbm.at[me_y], at2), (eet_hbm, eet), (cot_hbm, cot),
        ])
    ]
    for load in loads:
        load.start()

    barrier = pltpu.get_barrier_semaphore()
    for rel in (1, 2, 3):
        pl.semaphore_signal(barrier, inc=1, device_id=at_y(rel), device_id_type=MESH)

    def greet(d, carry):
        pl.semaphore_signal(barrier, inc=1, device_id=at_x(d), device_id_type=MESH)
        return carry

    lax.fori_loop(1, GX, greet, 0)
    pl.semaphore_signal(barrier, inc=1, device_id=twin, device_id_type=MESH)

    def remote(src, dst, ss, rs, dev):
        return pltpu.make_async_remote_copy(
            src_ref=src, dst_ref=dst, send_sem=ss, recv_sem=rs, device_id=dev, device_id_type=MESH
        )

    def rs_copy(t, i):
        src, dst, rel = [
            (part.at[2, 0], dg.at[t, 0], 1),
            (part.at[3, 0], fr.at[t, 0], 3),
            (part.at[1, 0], fl.at[t, 0], 1),
            (part.at[2, 1], dg.at[t, 1], 3),
            (part.at[1, 1], fl.at[t, 1], 1),
            (part.at[3, 1], fr.at[t, 1], 3),
        ][i]
        return remote(src, dst, rs_ss.at[t, i], rs_rs.at[t, i], at_y(rel))

    def ag_copy(t, i):
        src, dst, rel = [
            (ag.at[t, 0, 0], ag.at[t, 3, 0], 1),
            (ag.at[t, 0, 0], ag.at[t, 1, 0], 3),
            (ag.at[t, 3, 0], ag.at[t, 2, 0], 1),
            (ag.at[t, 0, 1], ag.at[t, 1, 1], 3),
            (ag.at[t, 0, 1], ag.at[t, 3, 1], 1),
            (ag.at[t, 1, 1], ag.at[t, 2, 1], 3),
        ][i]
        return remote(src, dst, ag_ss.at[t, i], ag_rs.at[t, i], at_y(rel))

    def h_copy(t, xc, d):
        to = lax.rem(me_x + d, GX)
        return remote(hs.at[xc, to], hr.at[t, xc, me_x], h_ss.at[t, xc, d], h_rs.at[t, xc, d], at_x(d))

    def b_copy(t, xc, d):
        to = lax.rem(me_x + d, GX)
        return remote(bs.at[xc, to], br.at[t, xc, me_x], b_ss.at[t, xc, d], b_rs.at[t, xc, d], at_x(d))

    def over_gx(fn):
        def step(d, carry):
            fn(d)
            return carry

        lax.fori_loop(1, GX, step, 0)

    def scale(jl):
        first = (me_y == 0) & (jl == 0)
        return jnp.where(first, 1.0, 2.0).astype(F32) * (1.0 / float(NX * NY * NZ))

    def forward_block(src, xc, rel):
        h = lax.rem(me_y + rel, GY)
        d = jnp.dot(src[xc * HALF:(xc + 1) * HALF, :], ee[h], preferred_element_type=F32).astype(BF16)
        for xp in range(4):
            r = xp * 128
            rhs = jnp.concatenate(
                [d[r:r + 64, :128], d[r:r + 64, 128:], d[r + 64:r + 128, :128], d[r + 64:r + 128, 128:]], 0
            )
            o = jnp.dot(a2[...], rhs, preferred_element_type=F32)
            part[rel, xc, xp * 192:(xp + 1) * 192, :] = o.astype(BF16)

    def add_part(rel, xc, other):
        part[rel, xc] = (part[rel, xc].astype(F32) + other.astype(F32)).astype(BF16)

    def sum_and_send(t, xc):
        s[...] = part[0, xc].astype(F32) + fl[t, xc].astype(F32) + fr[t, xc].astype(F32)

        def block(gx, carry):
            for k in range(3):
                r = gx * 3 + k
                top = s[pl.ds(r, 8, stride=96), :]
                low = s[pl.ds(r + KEPT, 8, stride=96), :]
                hs[xc, gx, k] = jnp.concatenate([top, low], 0).astype(BF16)
            return carry

        lax.fori_loop(0, GX, block, 0)
        over_gx(lambda d: h_copy(t, xc, d).start())
        hr[t, xc, me_x] = hs[xc, me_x]

    def x_transform(t, k, dst, index):
        hk = hr[t, :, :, k].reshape(512, 128)
        ht = lax.dot_general(pad[...], hk, NT, preferred_element_type=F32).astype(BF16)
        for n in range(4):
            dst[index, :, n * 512:(n + 1) * 512] = jnp.dot(
                ht, fx[:, n * 512:(n + 1) * 512], preferred_element_type=F32
            )

    def x_inverse_and_send(t):
        for xc in range(2):
            def block(k, carry):
                bx = lax.dot_general(fx[xc * 256:(xc + 1) * 256, :], lw[k], NT, preferred_element_type=F32)
                bx = jnp.dot(bx.astype(BF16), pad[...], preferred_element_type=F32).astype(BF16)
                bs[xc, :, k] = bx.reshape(GX, 16, 128)
                return carry

            lax.fori_loop(0, 3, block, 0)
            over_gx(lambda d: b_copy(t, xc, d).start())
            br[t, xc, me_x] = bs[xc, me_x]

    def gather_block(t, xc):
        over_gx(lambda d: b_copy(t, xc, d).wait_recv())

        def block(gx, carry):
            for k in range(3):
                r = gx * 3 + k
                v = br[t, xc, gx, k].astype(F32)
                s[pl.ds(r, 8, stride=96), :] = v[:8]
                s[pl.ds(r + KEPT, 8, stride=96), :] = v[8:]
            return carry

        lax.fori_loop(0, GX, block, 0)
        ag[t, 0, xc] = s[...].astype(BF16)

    def y_inverse(t, xc):
        def block(rel, carry):
            h = lax.rem(me_y + rel, GY)
            off = pl.multiple_of(h * 256, 256)
            for xp in range(4):
                v = jnp.dot(
                    at2[...], ag[t, rel, xc, xp * 192:(xp + 1) * 192, :], preferred_element_type=F32
                ).astype(BF16)
                for x2 in range(2):
                    rows = slice(xp * 128 + x2 * 64, xp * 128 + x2 * 64 + 64)
                    by[rows, pl.ds(off, 128)] = v[x2 * 128:x2 * 128 + 64]
                    by[rows, pl.ds(off + 128, 128)] = v[x2 * 128 + 64:x2 * 128 + 128]
            return carry

        lax.fori_loop(0, GY, block, 0)

    def depth_inverse(xc, finish):
        def block(n, carry):
            cols = pl.ds(pl.multiple_of(n * 256, 256), 256)
            for rb in range(2):
                rows = slice(xc * HALF + rb * 256, xc * HALF + rb * 256 + 256)
                v = jnp.dot(by[rb * 256:rb * 256 + 256, :], eet[:, cols], preferred_element_type=F32)
                finish(rows, cols, v + lin[rows, cols])
            return carry

        lax.fori_loop(0, 5, block, 0)

    def finish_forward(rows, cols, x):
        k0 = math.sqrt(2.0 / math.pi)
        x2 = x * x
        th = jnp.tanh(k0 * x * (1.0 + 0.044715 * x2))
        half = 0.5 * (1.0 + th)
        out[rows, cols] = (x * half).astype(BF16)
        slope = half + 0.5 * x * (1.0 - th * th) * (k0 * (1.0 + 3.0 * 0.044715 * x2))
        g[rows, cols] = (cot[rows, cols].astype(F32) * slope).astype(BF16)

    def finish_backward(rows, cols, x):
        out[rows, cols] = x.astype(BF16)

    def build_kron(ref):
        lane = lax.broadcasted_iota(jnp.int32, (NZ, CZ), 1) & (NZ - 1)
        row = lax.broadcasted_iota(jnp.int32, (NZ, CZ), 0)
        eye = jnp.where(lane == row, 1.0, 0.0).astype(F32)

        def block(c, carry):
            kron[pl.ds(pl.multiple_of(c * NZ, NZ), NZ), :] = (eye * ref[pl.ds(c, 1), :]).astype(BF16)
            return carry

        lax.fori_loop(0, C, block, 0)

    def linear(src):
        def block(n, carry):
            cols = pl.ds(pl.multiple_of(n * 256, 256), 256)
            for rb in range(2):
                rows = slice(rb * 512, rb * 512 + 512)
                lin[rows, cols] = jnp.dot(src[rows, :], kron[:, cols], preferred_element_type=F32)
            return carry

        lax.fori_loop(0, 5, block, 0)

    def fill_weights():
        wp[...] = jnp.zeros_like(wp)
        for k in range(3):
            def block(j, carry):
                for p in range(2):
                    wp[k, j, p, :C, :C * KEPT] = w_ref[k, j, p].astype(F32)
                return carry

            lax.fori_loop(0, 6, block, 0)
        lane = lax.broadcasted_iota(jnp.int32, (24, 1024), 1)
        first = lax.broadcasted_iota(jnp.int32, (24, 1024), 0) * KEPT
        mask[...] = jnp.where((lane >= first) & (lane < first + KEPT) & (lane < C * KEPT), 1.0, 0.0).astype(F32)

    def mix_block(k, carry):
        x_transform(0, k, uh, k)
        for jp in range(3):
            re, im = [], []
            for j in (2 * jp, 2 * jp + 1):
                a = uh[k, j * 24:(j + 1) * 24, :1024]
                b = uh[k, j * 24:(j + 1) * 24, 1024:]
                r, w = wp[k, j, 0], wp[k, j, 1]
                re.append(mask[...] * (jnp.sum(a * r - b * w, 0, keepdims=True) * scale(j)))
                im.append(mask[...] * (jnp.sum(a * w + b * r, 0, keepdims=True) * scale(j)))
            lw[k, jp * 48:(jp + 1) * 48, :1024] = jnp.concatenate(re, 0).astype(BF16)
            lw[k, jp * 48:(jp + 1) * 48, 1024:] = jnp.concatenate(im, 0).astype(BF16)
        return carry

    def adjoint_block(k, carry):
        x_transform(1, k, ut, 0)
        for jp in range(3):
            re, im = [], []
            for j in (2 * jp, 2 * jp + 1):
                r, w = wp[k, j, 0], wp[k, j, 1]
                gr = jnp.sum(ut[0, j * 24:(j + 1) * 24, :1024] * mask[...], 0, keepdims=True) * scale(j)
                gi = jnp.sum(ut[0, j * 24:(j + 1) * 24, 1024:] * mask[...], 0, keepdims=True) * scale(j)
                gh[k, j, 0:1, :] = gr
                gh[k, j, 1:2, :] = gi
                re.append(gr * r + gi * w)
                im.append(gi * r - gr * w)
            lw[k, jp * 48:(jp + 1) * 48, :1024] = jnp.concatenate(re, 0).astype(BF16)
            lw[k, jp * 48:(jp + 1) * 48, 1024:] = jnp.concatenate(im, 0).astype(BF16)
        return carry

    def weight_terms(k, j):
        rows = pl.ds(pl.multiple_of(j * 24, 8), 24)
        a, b = uh[k, rows, :1024], uh[k, rows, 1024:]
        gr, gi = gh[k, j, 0:1, :], gh[k, j, 1:2, :]
        return a * gr + b * gi, a * gi - b * gr

    def gs_copy():
        return remote(gss, gsr, gs_sem.at[0], gs_sem.at[1], twin)

    def weight_gradient_send():
        def block(k, carry):
            for jj in range(3):
                re, im = weight_terms(k, (1 - me_t) * 3 + jj)
                at = pl.multiple_of(k * 144 + jj * 48, 48)
                gss[pl.ds(at, 48), :] = jnp.concatenate([re, im], 0).astype(BF16)
            return carry

        lax.fori_loop(0, 3, block, 0)
        gs_copy().start()

    def weight_gradient_finish():
        gs_copy().wait_recv()

        def block(k, carry):
            for jj in range(3):
                re, im = weight_terms(k, me_t * 3 + jj)
                at = pl.multiple_of(k * 144 + jj * 48, 48)
                other = gsr[pl.ds(at, 48), :].astype(F32)
                gs_ref[k, jj, 0] = (re + other[:24])[:C, :C * KEPT]
                gs_ref[k, jj, 1] = (im + other[24:])[:C, :C * KEPT]
            return carry

        lax.fori_loop(0, 3, block, 0)

    def mixing_terms():
        lane = lax.broadcasted_iota(jnp.int32, (256, 256), 1) & (NZ - 1)
        row = lax.broadcasted_iota(jnp.int32, (256, 256), 0) & (NZ - 1)
        eye = jnp.where(lane == row, 1.0, 0.0).astype(F32)

        def block(cb, carry):
            cols = pl.ds(pl.multiple_of(cb * 256, 256), 256)
            for nb in range(5):
                o = lax.dot_general(
                    u[:, cols], g[:, nb * 256:(nb + 1) * 256], TN, preferred_element_type=F32
                )
                gmx[cb, 0:4, nb * 256:(nb + 1) * 256] = jnp.sum((o * eye).reshape(4, NZ, 256), 1)
            return carry

        gmx[...] = jnp.zeros_like(gmx)
        lax.fori_loop(0, 5, block, 0)
        v = gmx[...].reshape(40, CZ)
        hi = v.astype(BF16)
        low = (v - hi.astype(F32)).astype(BF16)
        sel = lax.broadcasted_iota(jnp.int32, (CZ, 128), 0) >> 6
        sel = jnp.where(sel == lax.broadcasted_iota(jnp.int32, (CZ, 128), 1), 1.0, 0.0).astype(BF16)
        gmy[0] = jnp.dot(hi, sel, preferred_element_type=F32) + jnp.dot(low, sel, preferred_element_type=F32)

    def gy_copy(rel):
        return remote(gmy.at[0], gmy.at[rel], gy_ss.at[rel], gy_rs.at[rel], at_y(rel))

    def gx_copy(d):
        return remote(gma.at[0], gma.at[d], gx_ss.at[d], gx_rs.at[d], at_x(d))

    def ta_copy():
        return remote(gma.at[16], gma.at[17], ta_sem.at[0], ta_sem.at[1], twin)

    pl.semaphore_wait(barrier, 19)
    for i in range(3):
        loads[i].wait()

    forward_block(u, 0, 2)
    rs_copy(0, 0).start()
    forward_block(u, 0, 3)
    rs_copy(0, 1).start()
    forward_block(u, 1, 2)
    rs_copy(0, 3).start()
    forward_block(u, 1, 1)
    rs_copy(0, 4).start()
    forward_block(u, 0, 1)
    forward_block(u, 1, 3)
    rs_copy(0, 0).wait_recv()
    add_part(1, 0, dg[0, 0])
    rs_copy(0, 2).start()
    rs_copy(0, 3).wait_recv()
    add_part(3, 1, dg[0, 1])
    rs_copy(0, 5).start()
    forward_block(u, 0, 0)
    forward_block(u, 1, 0)
    fill_weights()
    build_kron(mix_ref)
    linear(u)
    for i in range(3, 8):
        loads[i].wait()
    rs_copy(0, 1).wait_recv()
    rs_copy(0, 2).wait_recv()
    sum_and_send(0, 0)
    rs_copy(0, 4).wait_recv()
    rs_copy(0, 5).wait_recv()
    sum_and_send(0, 1)
    over_gx(lambda d: h_copy(0, 0, d).wait_recv())
    over_gx(lambda d: h_copy(0, 1, d).wait_recv())

    lax.fori_loop(0, 3, mix_block, 0)
    x_inverse_and_send(0)

    def gather(t):
        gather_block(t, 0)
        ag_copy(t, 0).start()
        ag_copy(t, 1).start()
        gather_block(t, 1)
        ag_copy(t, 3).start()
        ag_copy(t, 0).wait_recv()
        ag_copy(t, 2).start()
        ag_copy(t, 4).start()
        ag_copy(t, 3).wait_recv()
        ag_copy(t, 5).start()

    gather(0)
    for i in range(6):
        rs_copy(0, i).wait_send()
    for xc in range(2):
        over_gx(lambda d: h_copy(0, xc, d).wait_send())
        over_gx(lambda d: b_copy(0, xc, d).wait_send())

    ag_copy(0, 1).wait_recv()
    ag_copy(0, 2).wait_recv()
    y_inverse(0, 0)
    depth_inverse(0, finish_forward)
    act_out = [
        pltpu.make_async_copy(out.at[pl.ds(xc * HALF, HALF)], act_hbm.at[pl.ds(xc * HALF, HALF)], out_sem.at[0, xc])
        for xc in range(2)
    ]
    act_out[0].start()
    forward_block(g, 0, 2)
    rs_copy(1, 0).start()
    forward_block(g, 0, 3)
    rs_copy(1, 1).start()
    ag_copy(0, 4).wait_recv()
    ag_copy(0, 5).wait_recv()
    y_inverse(0, 1)
    depth_inverse(1, finish_forward)
    act_out[1].start()
    forward_block(g, 1, 2)
    rs_copy(1, 3).start()
    forward_block(g, 1, 1)
    rs_copy(1, 4).start()
    forward_block(g, 0, 1)
    rs_copy(1, 0).wait_recv()
    add_part(1, 0, dg[1, 0])
    rs_copy(1, 2).start()
    forward_block(g, 1, 3)
    rs_copy(1, 3).wait_recv()
    add_part(3, 1, dg[1, 1])
    rs_copy(1, 5).start()
    forward_block(g, 0, 0)
    forward_block(g, 1, 0)
    mixing_terms()
    for rel in (1, 2, 3):
        gy_copy(rel).start()
    rs_copy(1, 1).wait_recv()
    rs_copy(1, 2).wait_recv()
    sum_and_send(1, 0)
    rs_copy(1, 4).wait_recv()
    rs_copy(1, 5).wait_recv()
    sum_and_send(1, 1)
    for rel in (1, 2, 3):
        gy_copy(rel).wait_recv()
    gma[0] = gmy[0] + gmy[1] + gmy[2] + gmy[3]
    over_gx(lambda d: gx_copy(d).start())
    over_gx(lambda d: h_copy(1, 0, d).wait_recv())
    over_gx(lambda d: h_copy(1, 1, d).wait_recv())

    lax.fori_loop(0, 3, adjoint_block, 0)
    x_inverse_and_send(1)
    weight_gradient_send()
    gather(1)
    build_kron(mixt_ref)
    linear(g)
    over_gx(lambda d: gx_copy(d).wait_recv())
    gma[16] = jnp.sum(gma[0:16], 0)
    ta_copy().start()
    weight_gradient_finish()
    act_out[0].wait()
    act_out[1].wait()
    ag_copy(1, 1).wait_recv()
    ag_copy(1, 2).wait_recv()
    y_inverse(1, 0)
    depth_inverse(0, finish_backward)
    gf_out = [
        pltpu.make_async_copy(out.at[pl.ds(xc * HALF, HALF)], gf_hbm.at[pl.ds(xc * HALF, HALF)], out_sem.at[1, xc])
        for xc in range(2)
    ]
    gf_out[0].start()
    ag_copy(1, 4).wait_recv()
    ag_copy(1, 5).wait_recv()
    y_inverse(1, 1)
    depth_inverse(1, finish_backward)
    gf_out[1].start()
    ta_copy().wait_recv()
    total = (gma[16] + gma[17]) * (1.0 / math.sqrt(2 * NX * NY * NZ))
    for cb in range(5):
        gm_ref[cb * 4:(cb + 1) * 4, :] = total[cb * 8:cb * 8 + 4, :C]

    for t in range(2):
        for i in range(6):
            ag_copy(t, i).wait_send()
    for i in range(6):
        rs_copy(1, i).wait_send()
    for xc in range(2):
        over_gx(lambda d: h_copy(1, xc, d).wait_send())
        over_gx(lambda d: b_copy(1, xc, d).wait_send())
    gs_copy().wait_send()
    for rel in (1, 2, 3):
        gy_copy(rel).wait_send()
    over_gx(lambda d: gx_copy(d).wait_send())
    ta_copy().wait_send()
    gf_out[0].wait()
    gf_out[1].wait()


def shards(features, cotangent, spectral_weight, mixing_weight):
    mixing = mixing_weight.astype(F32)
    mix = jnp.repeat(mixing, NZ, axis=1)
    mixt = jnp.repeat(mixing.T, NZ, axis=1)
    consts = [jnp.asarray(t) for t in tables()]
    dma = pltpu.SemaphoreType.DMA
    vmem = pltpu.VMEM
    hbm = pl.BlockSpec(memory_space=pl.ANY)
    local = pl.BlockSpec(memory_space=pltpu.VMEM)
    act, gf, gs, gm = pl.pallas_call(
        kernel,
        out_shape=(
            jax.ShapeDtypeStruct((ROWS, CZ), BF16),
            jax.ShapeDtypeStruct((ROWS, CZ), BF16),
            jax.ShapeDtypeStruct((3, 3, 2, C, C * KEPT), F32),
            jax.ShapeDtypeStruct((C, C), F32),
        ),
        in_specs=[hbm, hbm, local, local, local] + [hbm] * 6,
        out_specs=(hbm, hbm, local, local),
        scratch_shapes=[
            vmem((ROWS, CZ), BF16),
            vmem((ROWS, CZ), BF16),
            vmem((ROWS, CZ), BF16),
            vmem((ROWS, CZ), BF16),
            vmem((GY, CZ, 256), BF16),
            vmem((GY * 256, CZ), BF16),
            vmem((CZ, CZ), BF16),
            vmem((ROWS, CZ), F32),
            vmem((512, 2048), BF16),
            vmem((144, 128), BF16),
            vmem((192, 256), BF16),
            vmem((256, 192), BF16),
            vmem((3, 6, 2, 24, 1024), F32),
            vmem((3, 144, 2048), F32),
            vmem((1, 144, 2048), F32),
            vmem((3, 144, 2048), BF16),
            vmem((432, 1024), BF16),
            vmem((432, 1024), BF16),
            vmem((4, 2, 768, 128), BF16),
            vmem((2, 2, 768, 128), BF16),
            vmem((2, 2, 768, 128), BF16),
            vmem((2, 2, 768, 128), BF16),
            vmem((2, GX, 3, 16, 128), BF16),
            vmem((2, 2, GX, 3, 16, 128), BF16),
            vmem((2, GX, 3, 16, 128), BF16),
            vmem((2, 2, GX, 3, 16, 128), BF16),
            vmem((2, 4, 2, 768, 128), BF16),
            vmem((HALF, 1024), BF16),
            vmem((768, 128), F32),
            vmem((24, 1024), F32),
            vmem((3, 6, 8, 1024), F32),
            vmem((5, 8, CZ), F32),
            vmem((4, 40, 128), F32),
            vmem((18, 40, 128), F32),
            dma((8,)),
            dma((2, 2)),
            dma((2, 6)),
            dma((2, 6)),
            dma((2, 2, GX)),
            dma((2, 2, GX)),
            dma((2, 2, GX)),
            dma((2, 2, GX)),
            dma((2, 6)),
            dma((2, 6)),
            dma((2,)),
            dma((4,)),
            dma((4,)),
            dma((GX,)),
            dma((GX,)),
            dma((2,)),
        ],
        compiler_params=pltpu.CompilerParams(
            collective_id=0, has_side_effects=True, vmem_limit_bytes=60 * 1024 * 1024
        ),
    )(
        features.reshape(ROWS, CZ), cotangent.reshape(ROWS, CZ), spectral_weight, mix, mixt, *consts,
    )
    return act.reshape(features.shape), gf.reshape(features.shape), gs, gm


def solution(mesh):
    in_specs = (
        P("ta", "gx", "gy", None),
        P("ta", "gx", "gy", None),
        P("gx", "gy", None, None, None),
        P(),
    )
    out_specs = (
        P("ta", "gx", "gy", None),
        P("ta", "gx", "gy", None),
        P("gx", ("gy", "ta"), None, None, None),
        P(),
    )
    return jax.shard_map(shards, mesh=mesh, in_specs=in_specs, out_specs=out_specs, check_vma=False)
```

profile of v0, /device:TPU:0, one launch (start us, length us, event | category | flops | bytes accessed | tf_op | source)
XLA Modules:
  0.0 142.6 jit_solution(2671786352314242893)
XLA Ops:
  0.6 0.7 convert_bitcast_fusion
  1.3 0.1 copy.14
  1.4 0.1 broadcast_in_dim.7
  1.5 0.8 reshape.29.mixt_ref
  2.3 0.8 broadcast_in_dim.6
  3.1 0.8 reshape.28.mix_ref
  3.9 3.1 %copy.15.w_ref = bf16[3,6,2,20,960]{4,3,2,1,0:T(8,128)(2,1)} copy(bf16[3,6,2,20,960]{4,2,3,1,0:T(2,128)(2,1)} %param.12) | data formatting | bytes 2764800 | tf_op args[2]
  7.0 127.0 %shard_map.129 = (bf16[1024,1280]{1,0:T(8,128)(2,1)}, bf16[1024,1280]{1,0:T(8,128)(2,1)}, f32[3,3,2,20,960]{4,3,2,1,0:T(8,128)}, f32[20,20]{1,0:T(8,128)}) custom-call(bf16[1024,1280]{1,0:T(8,128)(2,1)} %bitcast.6, bf16[1024,1280]{1,0:T(8,128)(2,1)} %bitcast.7, bf16[3,6,2,20,960]{4,3,2,1,0:T(8,128)(2,1)} %copy.15.w_ref, f32[20,1280]{1,0:T(8,128)} %reshape.28.mix_ref, ...), custom_call_target="tpu_custom_call" | custom-call | tf_op jit(solution)/shard_map/pallas_call | solution.py:553
  133.9 0.0 copy-start.1
  133.9 3.9 %copy.16 = f32[3,3,2,20,960]{4,2,3,1,0:T(2,128)} copy(f32[3,3,2,20,960]{4,3,2,1,0:T(8,128)} %get-tuple-element.14) | data formatting | bytes 2764800
  137.8 0.0 copy-done.1
  137.8 0.0 copy-start
  137.8 1.5 %copy.20 = bf16[1,16,64,1280]{3,2,1,0:T(8,128)(2,1)} copy(bf16[1,16,64,1280]{3,2,1,0:T(8,128)(2,1)S(1)} %bitcast.9) | data formatting | bytes 5242880
  139.3 1.2 copy-done
  140.5 0.0 copy-start.2
  140.5 1.5 %copy.21 = bf16[1,16,64,1280]{3,2,1,0:T(8,128)(2,1)} copy(bf16[1,16,64,1280]{3,2,1,0:T(8,128)(2,1)S(1)} %bitcast.8) | data formatting | bytes 5242880
  142.0 0.0 copy-done.2
  142.0 0.6 copy.22
Async XLA Ops:
  133.9 3.9 %copy-start.1 = (bf16[1024,1280]{1,0:T(8,128)(2,1)S(1)}, bf16[1024,1280]{1,0:T(8,128)(2,1)}, u32[]{:S(2)}) copy-start(bf16[1024,1280]{1,0:T(8,128)(2,1)} %get-tuple-element.8) | copy-start | bytes 7864324
  137.8 2.7 %copy-start = (bf16[1024,1280]{1,0:T(8,128)(2,1)S(1)}, bf16[1024,1280]{1,0:T(8,128)(2,1)}, u32[]{:S(2)}) copy-start(bf16[1024,1280]{1,0:T(8,128)(2,1)} %get-tuple-element.9) | copy-start | bytes 7864324
  140.5 1.5 %copy-start.2 = (f32[20,20]{1,0:T(8,128)S(1)}, f32[20,20]{1,0:T(8,128)}, u32[]{:S(2)}) copy-start(f32[20,20]{1,0:T(8,128)} %get-tuple-element.23) | copy-start | bytes 4804
where the time goes:
time: 143 us
  Pallas kernels  127 us (89%)
  local copies, waits for them, and re-layouts  14.3 us (10%)
    pallas_call x1, Pallas kernels, shards(): pl.pallas_call(kernel, out_shape=(jax.ShapeDtypeStruct((ROWS, CZ), BF16),...  127 us
    unnamed x11, local copies, waits for them, and re-layouts  11.7 us

commit v1 on v0

--- a/solution.py
+++ b/solution.py
@@ -58,21 +58,26 @@
     a2 = a2.reshape(GY, 192, 256)
     at2 = np.ascontiguousarray(a2.transpose(0, 2, 1))
     width = complex_table(NX, KEPT).reshape(2, GX, 2, 8, 2, KEPT)
-    fx = np.zeros((2, GX, 2, 8, 2, 1024), np.float32)
-    fx[..., : C * KEPT] = np.tile(width.transpose(2, 1, 0, 3, 4, 5), (1, 1, 1, 1, 1, C))
-    fx = fx.reshape(512, 2048)
+    fx = np.zeros((2, GX, 2, 8, 2, 128), np.float32)
+    fx[..., :KEPT] = width.transpose(2, 1, 0, 3, 4, 5)
+    fx = fx.reshape(512, 256)
+    spread = np.zeros((128, 1024), np.float32)
+    for c in range(C):
+        spread[np.arange(KEPT), c * KEPT + np.arange(KEPT)] = 1.0
+    fold = np.ascontiguousarray(spread.T)
     pad = np.zeros((6, 24, 128), np.float32)
     for jl in range(6):
         for c in range(C):
             pad[jl, c, jl * C + c] = 1.0
     pad = pad.reshape(144, 128)
-    return [t.astype(ml_dtypes.bfloat16) for t in (ee, eet, a2, at2, fx, pad)]
+    padt = np.ascontiguousarray(pad.T)
+    return [t.astype(ml_dtypes.bfloat16) for t in (ee, eet, a2, at2, fx, pad, padt, spread, fold)]
 
 
 def kernel(
-    u_hbm, cot_hbm, w_ref, mix_ref, mixt_ref, ee_hbm, eet_hbm, a2_hbm, at2_hbm, fx_hbm, pad_hbm,
+    u_hbm, cot_hbm, w_hbm, mix_ref, ee_hbm, eet_hbm, a2_hbm, at2_hbm, fx_hbm, pad_hbm, padt_hbm, spread_hbm, fold_hbm,
     act_hbm, gf_hbm, gs_ref, gm_ref,
-    u, cot, g, out, ee, eet, kron, lin, fx, pad, a2, at2, wp, uh, ut, lw, gss, gsr,
+    u, cot, g, out, ee, eet, kron, lin, fx, pad, padt, spread, fold, a2, at2, w, mixrows, wp, uh, ht, yk, lw, gss, gsr,
     part, dg, fl, fr, hs, hr, bs, br, ag, by, s, mask, gh, gmx, gmy, gma,
     in_sem, out_sem, rs_ss, rs_rs, h_ss, h_rs, b_ss, b_rs, ag_ss, ag_rs, gs_sem, gy_ss, gy_rs, gx_ss, gx_rs, ta_sem,
 ):
@@ -88,11 +93,16 @@
 
     twin = (me_x, me_y, 1 - me_t)
 
+    opposite, left = lax.rem(me_y + 2, GY), lax.rem(me_y + 3, GY)
+    right = lax.rem(me_y + 1, GY)
+    first, second = pl.ds(0, HALF), pl.ds(HALF, HALF)
     loads = [
         pltpu.make_async_copy(src, dst, in_sem.at[i])
         for i, (src, dst) in enumerate([
-            (u_hbm, u), (ee_hbm, ee), (a2_hbm.at[me_y], a2), (fx_hbm, fx), (pad_hbm, pad),
-            (at2_hbm.at[me_y], at2), (eet_hbm, eet), (cot_hbm, cot),
+            (u_hbm.at[first], u.at[first]), (ee_hbm.at[opposite], ee.at[opposite]), (a2_hbm.at[me_y], a2),
+            (ee_hbm.at[left], ee.at[left]), (u_hbm.at[second], u.at[second]), (ee_hbm.at[right], ee.at[right]),
+            (ee_hbm.at[me_y], ee.at[me_y]), (w_hbm, w), (fx_hbm, fx), (pad_hbm, pad), (padt_hbm, padt),
+            (spread_hbm, spread), (fold_hbm, fold), (at2_hbm.at[me_y], at2), (eet_hbm, eet), (cot_hbm, cot),
         ])
     ]
     for load in loads:
@@ -184,23 +194,28 @@
         over_gx(lambda d: h_copy(t, xc, d).start())
         hr[t, xc, me_x] = hs[xc, me_x]
 
-    def x_transform(t, k, dst, index):
-        hk = hr[t, :, :, k].reshape(512, 128)
-        ht = lax.dot_general(pad[...], hk, NT, preferred_element_type=F32).astype(BF16)
-        for n in range(4):
-            dst[index, :, n * 512:(n + 1) * 512] = jnp.dot(
-                ht, fx[:, n * 512:(n + 1) * 512], preferred_element_type=F32
-            )
+    def x_transform(t, put):
+        for k in range(3):
+            hk = hr[t, :, :, k].reshape(512, 128)
+            ht[k * 144:(k + 1) * 144, :] = lax.dot_general(
+                pad[...], hk, NT, preferred_element_type=F32
+            ).astype(BF16)
+        v = jnp.dot(ht[...], fx[...], preferred_element_type=F32).astype(BF16)
+        for q in range(2):
+            for n in range(2):
+                put(q, n * 512, jnp.dot(
+                    v[:, q * 128:(q + 1) * 128], spread[:, n * 512:(n + 1) * 512], preferred_element_type=F32
+                ))
 
     def x_inverse_and_send(t):
+        y = jnp.dot(lw[...], fold[...], preferred_element_type=F32).astype(BF16)
+        for k in range(3):
+            both = jnp.concatenate([y[k * 144:(k + 1) * 144], y[432 + k * 144:432 + (k + 1) * 144]], 1)
+            yk[k] = jnp.dot(padt[...], both, preferred_element_type=F32).astype(BF16)
         for xc in range(2):
-            def block(k, carry):
-                bx = lax.dot_general(fx[xc * 256:(xc + 1) * 256, :], lw[k], NT, preferred_element_type=F32)
-                bx = jnp.dot(bx.astype(BF16), pad[...], preferred_element_type=F32).astype(BF16)
-                bs[xc, :, k] = bx.reshape(GX, 16, 128)
-                return carry
-
-            lax.fori_loop(0, 3, block, 0)
+            for k in range(3):
+                bx = lax.dot_general(fx[xc * 256:(xc + 1) * 256, :], yk[k], NT, preferred_element_type=F32)
+                bs[xc, :, k] = bx.astype(BF16).reshape(GX, 16, 128)
             over_gx(lambda d: b_copy(t, xc, d).start())
             br[t, xc, me_x] = bs[xc, me_x]
 
@@ -234,7 +249,7 @@
 
         lax.fori_loop(0, GY, block, 0)
 
-    def depth_inverse(xc, finish):
+    def depth_inverse(xc, finish, start=0, stop=5):
         def block(n, carry):
             cols = pl.ds(pl.multiple_of(n * 256, 256), 256)
             for rb in range(2):
@@ -243,7 +258,7 @@
                 finish(rows, cols, v + lin[rows, cols])
             return carry
 
-        lax.fori_loop(0, 5, block, 0)
+        lax.fori_loop(start, stop, block, 0)
 
     def finish_forward(rows, cols, x):
         k0 = math.sqrt(2.0 / math.pi)
@@ -257,23 +272,26 @@
     def finish_backward(rows, cols, x):
         out[rows, cols] = x.astype(BF16)
 
-    def build_kron(ref):
+    def build_kron(dims):
+        at = lax.broadcasted_iota(jnp.int32, (C, CZ), 1) >> 6
+        one = jnp.where(at == lax.broadcasted_iota(jnp.int32, (C, CZ), 0), 1.0, 0.0).astype(BF16)
+        mixrows[...] = lax.dot_general(mix_ref[...], one, dims, preferred_element_type=F32)
+
         lane = lax.broadcasted_iota(jnp.int32, (NZ, CZ), 1) & (NZ - 1)
         row = lax.broadcasted_iota(jnp.int32, (NZ, CZ), 0)
         eye = jnp.where(lane == row, 1.0, 0.0).astype(F32)
 
         def block(c, carry):
-            kron[pl.ds(pl.multiple_of(c * NZ, NZ), NZ), :] = (eye * ref[pl.ds(c, 1), :]).astype(BF16)
+            kron[pl.ds(pl.multiple_of(c * NZ, NZ), NZ), :] = (eye * mixrows[pl.ds(c, 1), :]).astype(BF16)
             return carry
 
         lax.fori_loop(0, C, block, 0)
 
-    def linear(src):
+    def linear(src, rb):
         def block(n, carry):
             cols = pl.ds(pl.multiple_of(n * 256, 256), 256)
-            for rb in range(2):
-                rows = slice(rb * 512, rb * 512 + 512)
-                lin[rows, cols] = jnp.dot(src[rows, :], kron[:, cols], preferred_element_type=F32)
+            rows = slice(rb * 512, rb * 512 + 512)
+            lin[rows, cols] = jnp.dot(src[rows, :], kron[:, cols], preferred_element_type=F32)
             return carry
 
         lax.fori_loop(0, 5, block, 0)
@@ -282,8 +300,9 @@
         wp[...] = jnp.zeros_like(wp)
         for k in range(3):
             def block(j, carry):
+                v = w[k, j].astype(F32)
                 for p in range(2):
-                    wp[k, j, p, :C, :C * KEPT] = w_ref[k, j, p].astype(F32)
+                    wp[k, j, p, :C, :C * KEPT] = v[:, p, :]
                 return carry
 
             lax.fori_loop(0, 6, block, 0)
@@ -291,39 +310,47 @@
         first = lax.broadcasted_iota(jnp.int32, (24, 1024), 0) * KEPT
         mask[...] = jnp.where((lane >= first) & (lane < first + KEPT) & (lane < C * KEPT), 1.0, 0.0).astype(F32)
 
+    def put_uh(q, at, v):
+        uh[q, :, at:at + 512] = v
+
+    def put_lin(q, at, v):
+        lin[q * 432:(q + 1) * 432, at:at + 512] = v
+
+    def put_rows(k, jp, re, im):
+        at = pl.multiple_of(k * 144 + jp * 48, 48)
+        lw[pl.ds(at, 48), :] = jnp.concatenate(re, 0).astype(BF16)
+        lw[pl.ds(at + 432, 48), :] = jnp.concatenate(im, 0).astype(BF16)
+
     def mix_block(k, carry):
-        x_transform(0, k, uh, k)
         for jp in range(3):
             re, im = [], []
             for j in (2 * jp, 2 * jp + 1):
-                a = uh[k, j * 24:(j + 1) * 24, :1024]
-                b = uh[k, j * 24:(j + 1) * 24, 1024:]
+                rows = pl.ds(pl.multiple_of(k * 144 + j * 24, 8), 24)
+                a, b = uh[0, rows, :], uh[1, rows, :]
                 r, w = wp[k, j, 0], wp[k, j, 1]
                 re.append(mask[...] * (jnp.sum(a * r - b * w, 0, keepdims=True) * scale(j)))
                 im.append(mask[...] * (jnp.sum(a * w + b * r, 0, keepdims=True) * scale(j)))
-            lw[k, jp * 48:(jp + 1) * 48, :1024] = jnp.concatenate(re, 0).astype(BF16)
-            lw[k, jp * 48:(jp + 1) * 48, 1024:] = jnp.concatenate(im, 0).astype(BF16)
+            put_rows(k, jp, re, im)
         return carry
 
     def adjoint_block(k, carry):
-        x_transform(1, k, ut, 0)
         for jp in range(3):
             re, im = [], []
             for j in (2 * jp, 2 * jp + 1):
+                at = pl.multiple_of(k * 144 + j * 24, 8)
                 r, w = wp[k, j, 0], wp[k, j, 1]
-                gr = jnp.sum(ut[0, j * 24:(j + 1) * 24, :1024] * mask[...], 0, keepdims=True) * scale(j)
-                gi = jnp.sum(ut[0, j * 24:(j + 1) * 24, 1024:] * mask[...], 0, keepdims=True) * scale(j)
+                gr = jnp.sum(lin[pl.ds(at, 24), :1024] * mask[...], 0, keepdims=True) * scale(j)
+                gi = jnp.sum(lin[pl.ds(at + 432, 24), :1024] * mask[...], 0, keepdims=True) * scale(j)
                 gh[k, j, 0:1, :] = gr
                 gh[k, j, 1:2, :] = gi
                 re.append(gr * r + gi * w)
                 im.append(gi * r - gr * w)
-            lw[k, jp * 48:(jp + 1) * 48, :1024] = jnp.concatenate(re, 0).astype(BF16)
-            lw[k, jp * 48:(jp + 1) * 48, 1024:] = jnp.concatenate(im, 0).astype(BF16)
+            put_rows(k, jp, re, im)
         return carry
 
     def weight_terms(k, j):
-        rows = pl.ds(pl.multiple_of(j * 24, 8), 24)
-        a, b = uh[k, rows, :1024], uh[k, rows, 1024:]
+        rows = pl.ds(pl.multiple_of(k * 144 + j * 24, 8), 24)
+        a, b = uh[0, rows, :], uh[1, rows, :]
         gr, gi = gh[k, j, 0:1, :], gh[k, j, 1:2, :]
         return a * gr + b * gi, a * gi - b * gr
 
@@ -349,8 +376,8 @@
                 re, im = weight_terms(k, me_t * 3 + jj)
                 at = pl.multiple_of(k * 144 + jj * 48, 48)
                 other = gsr[pl.ds(at, 48), :].astype(F32)
-                gs_ref[k, jj, 0] = (re + other[:24])[:C, :C * KEPT]
-                gs_ref[k, jj, 1] = (im + other[24:])[:C, :C * KEPT]
+                gs_ref[k, jj, :, 0, :] = (re + other[:24])[:C, :C * KEPT]
+                gs_ref[k, jj, :, 1, :] = (im + other[24:])[:C, :C * KEPT]
             return carry
 
         lax.fori_loop(0, 3, block, 0)
@@ -387,32 +414,35 @@
     def ta_copy():
         return remote(gma.at[16], gma.at[17], ta_sem.at[0], ta_sem.at[1], twin)
 
-    pl.semaphore_wait(barrier, 19)
     for i in range(3):
         loads[i].wait()
-
     forward_block(u, 0, 2)
+    pl.semaphore_wait(barrier, 19)
     rs_copy(0, 0).start()
+    loads[3].wait()
     forward_block(u, 0, 3)
     rs_copy(0, 1).start()
+    loads[4].wait()
     forward_block(u, 1, 2)
     rs_copy(0, 3).start()
+    loads[5].wait()
     forward_block(u, 1, 1)
     rs_copy(0, 4).start()
     forward_block(u, 0, 1)
-    forward_block(u, 1, 3)
+    loads[6].wait()
+    forward_block(u, 0, 0)
     rs_copy(0, 0).wait_recv()
     add_part(1, 0, dg[0, 0])
     rs_copy(0, 2).start()
+    forward_block(u, 1, 3)
     rs_copy(0, 3).wait_recv()
     add_part(3, 1, dg[0, 1])
     rs_copy(0, 5).start()
-    forward_block(u, 0, 0)
     forward_block(u, 1, 0)
+    loads[7].wait()
     fill_weights()
-    build_kron(mix_ref)
-    linear(u)
-    for i in range(3, 8):
+    build_kron((((1,), (0,)), ((), ())))
+    for i in range(8, 16):
         loads[i].wait()
     rs_copy(0, 1).wait_recv()
     rs_copy(0, 2).wait_recv()
@@ -423,22 +453,25 @@
     over_gx(lambda d: h_copy(0, 0, d).wait_recv())
     over_gx(lambda d: h_copy(0, 1, d).wait_recv())
 
+    x_transform(0, put_uh)
     lax.fori_loop(0, 3, mix_block, 0)
     x_inverse_and_send(0)
 
-    def gather(t):
+    def gather(t, src):
         gather_block(t, 0)
         ag_copy(t, 0).start()
         ag_copy(t, 1).start()
         gather_block(t, 1)
         ag_copy(t, 3).start()
+        linear(src, 0)
         ag_copy(t, 0).wait_recv()
         ag_copy(t, 2).start()
         ag_copy(t, 4).start()
         ag_copy(t, 3).wait_recv()
         ag_copy(t, 5).start()
-
-    gather(0)
+        linear(src, 1)
+
+    gather(0, u)
     for i in range(6):
         rs_copy(0, i).wait_send()
     for xc in range(2):
@@ -458,25 +491,26 @@
     rs_copy(1, 0).start()
     forward_block(g, 0, 3)
     rs_copy(1, 1).start()
+    forward_block(g, 0, 1)
     ag_copy(0, 4).wait_recv()
     ag_copy(0, 5).wait_recv()
     y_inverse(0, 1)
-    depth_inverse(1, finish_forward)
+    depth_inverse(1, finish_forward, 0, 3)
+    rs_copy(1, 0).wait_recv()
+    add_part(1, 0, dg[1, 0])
+    rs_copy(1, 2).start()
+    depth_inverse(1, finish_forward, 3, 5)
     act_out[1].start()
     forward_block(g, 1, 2)
     rs_copy(1, 3).start()
     forward_block(g, 1, 1)
     rs_copy(1, 4).start()
-    forward_block(g, 0, 1)
-    rs_copy(1, 0).wait_recv()
-    add_part(1, 0, dg[1, 0])
-    rs_copy(1, 2).start()
     forward_block(g, 1, 3)
+    forward_block(g, 0, 0)
+    forward_block(g, 1, 0)
     rs_copy(1, 3).wait_recv()
     add_part(3, 1, dg[1, 1])
     rs_copy(1, 5).start()
-    forward_block(g, 0, 0)
-    forward_block(g, 1, 0)
     mixing_terms()
     for rel in (1, 2, 3):
         gy_copy(rel).start()
@@ -493,12 +527,12 @@
     over_gx(lambda d: h_copy(1, 0, d).wait_recv())
     over_gx(lambda d: h_copy(1, 1, d).wait_recv())
 
+    x_transform(1, put_lin)
     lax.fori_loop(0, 3, adjoint_block, 0)
     x_inverse_and_send(1)
     weight_gradient_send()
-    gather(1)
-    build_kron(mixt_ref)
-    linear(g)
+    build_kron(TN)
+    gather(1, g)
     over_gx(lambda d: gx_copy(d).wait_recv())
     gma[16] = jnp.sum(gma[0:16], 0)
     ta_copy().start()
@@ -541,24 +575,39 @@
     gf_out[1].wait()
 
 
+def hand_over(act_in, gf_in, gs_in, gm_in, act_out, gf_out, gs_out, gm_out, act, gf, gs, gm, in_sem, out_sem):
+    pieces = [(gs_in.at[k], gs.at[k], gs_out.at[k]) for k in range(3)] + [(gm_in, gm, gm_out)]
+    for i in range(4):
+        rows = pl.ds(i * 256, 256)
+        pieces.append((act_in.at[rows], act.at[rows], act_out.at[rows]))
+        pieces.append((gf_in.at[rows], gf.at[rows], gf_out.at[rows]))
+    loads = [pltpu.make_async_copy(p[0], p[1], in_sem.at[i]) for i, p in enumerate(pieces)]
+    stores = [pltpu.make_async_copy(p[1], p[2], out_sem.at[i]) for i, p in enumerate(pieces)]
+    for load in loads:
+        load.start()
+    for load, store in zip(loads, stores):
+        load.wait()
+        store.start()
+    for store in stores:
+        store.wait()
+
+
 def shards(features, cotangent, spectral_weight, mixing_weight):
-    mixing = mixing_weight.astype(F32)
-    mix = jnp.repeat(mixing, NZ, axis=1)
-    mixt = jnp.repeat(mixing.T, NZ, axis=1)
     consts = [jnp.asarray(t) for t in tables()]
     dma = pltpu.SemaphoreType.DMA
     vmem = pltpu.VMEM
     hbm = pl.BlockSpec(memory_space=pl.ANY)
     local = pl.BlockSpec(memory_space=pltpu.VMEM)
-    act, gf, gs, gm = pl.pallas_call(
+    results = (
+        jax.ShapeDtypeStruct((ROWS, CZ), BF16),
+        jax.ShapeDtypeStruct((ROWS, CZ), BF16),
+        jax.ShapeDtypeStruct((3, 3, C, 2, C * KEPT), F32),
+        jax.ShapeDtypeStruct((C, C), F32),
+    )
+    parts = pl.pallas_call(
         kernel,
-        out_shape=(
-            jax.ShapeDtypeStruct((ROWS, CZ), BF16),
-            jax.ShapeDtypeStruct((ROWS, CZ), BF16),
-            jax.ShapeDtypeStruct((3, 3, 2, C, C * KEPT), F32),
-            jax.ShapeDtypeStruct((C, C), F32),
-        ),
-        in_specs=[hbm, hbm, local, local, local] + [hbm] * 6,
+        out_shape=results,
+        in_specs=[hbm, hbm, hbm, local] + [hbm] * 9,
         out_specs=(hbm, hbm, local, local),
         scratch_shapes=[
             vmem((ROWS, CZ), BF16),
@@ -569,14 +618,20 @@
             vmem((GY * 256, CZ), BF16),
             vmem((CZ, CZ), BF16),
             vmem((ROWS, CZ), F32),
-            vmem((512, 2048), BF16),
+            vmem((512, 256), BF16),
             vmem((144, 128), BF16),
+            vmem((128, 144), BF16),
+            vmem((128, 1024), BF16),
+            vmem((1024, 128), BF16),
             vmem((192, 256), BF16),
             vmem((256, 192), BF16),
+            vmem((3, 6, C, 2, C * KEPT), BF16),
+            vmem((C, CZ), F32),
             vmem((3, 6, 2, 24, 1024), F32),
-            vmem((3, 144, 2048), F32),
-            vmem((1, 144, 2048), F32),
-            vmem((3, 144, 2048), BF16),
+            vmem((2, 432, 1024), F32),
+            vmem((432, 512), BF16),
+            vmem((3, 128, 256), BF16),
+            vmem((864, 1024), BF16),
             vmem((432, 1024), BF16),
             vmem((432, 1024), BF16),
             vmem((4, 2, 768, 128), BF16),
@@ -595,7 +650,7 @@
             vmem((5, 8, CZ), F32),
             vmem((4, 40, 128), F32),
             vmem((18, 40, 128), F32),
-            dma((8,)),
+            dma((16,)),
             dma((2, 2)),
             dma((2, 6)),
             dma((2, 6)),
@@ -616,9 +671,18 @@
             collective_id=0, has_side_effects=True, vmem_limit_bytes=60 * 1024 * 1024
         ),
     )(
-        features.reshape(ROWS, CZ), cotangent.reshape(ROWS, CZ), spectral_weight, mix, mixt, *consts,
+        features.reshape(ROWS, CZ), cotangent.reshape(ROWS, CZ),
+        spectral_weight.transpose(0, 1, 3, 2, 4), mixing_weight, *consts,
     )
-    return act.reshape(features.shape), gf.reshape(features.shape), gs, gm
+    act, gf, gs, gm = pl.pallas_call(
+        hand_over,
+        out_shape=results,
+        in_specs=[hbm] * 4,
+        out_specs=(hbm,) * 4,
+        scratch_shapes=[vmem(r.shape, r.dtype) for r in results] + [dma((12,)), dma((12,))],
+        compiler_params=pltpu.CompilerParams(vmem_limit_bytes=60 * 1024 * 1024),
+    )(*parts)
+    return act.reshape(features.shape), gf.reshape(features.shape), gs.transpose(0, 1, 3, 2, 4), gm
 
 
 def solution(mesh):

time: 143 us -> 126 us (0.88)
  local copies, waits for them, and re-layouts: 14.3 us -> 0 us
  Pallas kernels: 127 us -> 124 us
    unnamed x11 -> x0, local copies, waits for them, and re-layouts: 11.7 us -> none
    pallas_call x1 -> x2, Pallas kernels: 127 us -> 124 us  [the longest x1 118 us: shards(): pl.pallas_call(kernel, out_shape=results, in_specs=[hbm, hbm, hbm, local]...]
    reshape x2 -> x0, local copies, waits for them, and re-layouts: 1.53 us -> none  [the longest x1 0.76 us: shards(): mixt = jnp.repeat(mixing.T, NZ, axis=1)]
where the time goes in v1:
time: 126 us; the launch traced here: 125 us
  Pallas kernels  124 us (98%)
    pallas_call x1, Pallas kernels, shards(): pl.pallas_call(kernel, out_shape=results, in_specs=[hbm, hbm, hbm, local]...  118 us
    pallas_call x1, Pallas kernels, shards(): pl.pallas_call(hand_over, out_shape=results, in_specs=[hbm] * 4, out_spec...  5.69 us

profile of v1, /device:TPU:0, one launch (start us, length us, event | category | flops | bytes accessed | tf_op | source)
XLA Modules:
  0.0 124.8 jit_solution(3938202093228605192)
XLA Ops:
  0.6 118.3 %shard_map.156 = (bf16[1024,1280]{1,0:T(8,128)(2,1)}, bf16[1024,1280]{1,0:T(8,128)(2,1)}, f32[3,3,20,2,960]{4,3,2,1,0:T(2,128)}, f32[20,20]{1,0:T(8,128)}) custom-call(bf16[1024,1280]{1,0:T(8,128)(2,1)} %bitcast.6, bf16[1024,1280]{1,0:T(8,128)(2,1)} %bitcast.7, bf16[3,6,20,2,960]{4,3,2,1,0:T(2,128)(2,1)} %bitcast.8, bf16[20,20]{1,0:T(8,128)(2,1)} %mix_ref.1, ...), custom_call_target="tpu_custom_call" | custom-call | tf_op jit(solution)/shard_map/pallas_call | solution.py:607
  118.9 5.7 %shard_map.157 = (bf16[1024,1280]{1,0:T(8,128)(2,1)}, bf16[1024,1280]{1,0:T(8,128)(2,1)}, f32[3,3,20,2,960]{4,3,2,1,0:T(2,128)}, f32[20,20]{1,0:T(8,128)}) custom-call(bf16[1024,1280]{1,0:T(8,128)(2,1)} %get-tuple-element.12.act_in, bf16[1024,1280]{1,0:T(8,128)(2,1)} %get-tuple-element.13.gf_in, f32[3,3,20,2,960]{4,3,2,1,0:T(2,128)} %get-tuple-element.14.gs_in, ...), custom_call_target="tpu_custom_call" | custom-call | tf_op jit(solution)/shard_map/pallas_call | solution.py:677

commit v2 on v1

--- a/solution.py
+++ b/solution.py
@@ -52,19 +52,22 @@
     ee = ee.reshape(GY, CZ, 256)
     eet = np.ascontiguousarray(ee.transpose(0, 2, 1)).reshape(GY * 256, CZ)
     height = complex_table(NY, KEPT).reshape(2, GY, 64, 2, KEPT)
-    a2 = np.zeros((GY, 2, 2, KEPT, 2, 2, 64), np.float32)
+    height = height.transpose(1, 3, 4, 0, 2).reshape(GY, 2, GX, 3, 2, 64)
+    a2 = np.zeros((GY, 192, 2, 2, 64), np.float32)
     for x2 in range(2):
-        a2[:, x2, :, :, x2] = height.transpose(1, 3, 4, 0, 2)
+        a2[:, x2 * 64:x2 * 64 + 64, x2] = height[:, :, :, :2].reshape(GY, 64, 2, 64)
+        a2[:, 128 + x2 * 32:160 + x2 * 32, x2] = height[:, :, :, 2].reshape(GY, 32, 2, 64)
     a2 = a2.reshape(GY, 192, 256)
     at2 = np.ascontiguousarray(a2.transpose(0, 2, 1))
     width = complex_table(NX, KEPT).reshape(2, GX, 2, 8, 2, KEPT)
-    fx = np.zeros((2, GX, 2, 8, 2, 128), np.float32)
+    fx = np.zeros((2, GX, 2, 8, 2, 64), np.float32)
     fx[..., :KEPT] = width.transpose(2, 1, 0, 3, 4, 5)
-    fx = fx.reshape(512, 256)
-    spread = np.zeros((128, 1024), np.float32)
-    for c in range(C):
-        spread[np.arange(KEPT), c * KEPT + np.arange(KEPT)] = 1.0
-    fold = np.ascontiguousarray(spread.T)
+    fx = fx.reshape(512, 128)
+    spread = np.zeros((2, 128, 1024), np.float32)
+    for q in range(2):
+        for c in range(C):
+            spread[q, q * 64 + np.arange(KEPT), c * KEPT + np.arange(KEPT)] = 1.0
+    fold = np.ascontiguousarray(spread.transpose(0, 2, 1))
     pad = np.zeros((6, 24, 128), np.float32)
     for jl in range(6):
         for c in range(C):
@@ -78,8 +81,9 @@
     u_hbm, cot_hbm, w_hbm, mix_ref, ee_hbm, eet_hbm, a2_hbm, at2_hbm, fx_hbm, pad_hbm, padt_hbm, spread_hbm, fold_hbm,
     act_hbm, gf_hbm, gs_ref, gm_ref,
     u, cot, g, out, ee, eet, kron, lin, fx, pad, padt, spread, fold, a2, at2, w, mixrows, wp, uh, ht, yk, lw, gss, gsr,
-    part, dg, fl, fr, hs, hr, bs, br, ag, by, s, mask, gh, gmx, gmy, gma,
-    in_sem, out_sem, rs_ss, rs_rs, h_ss, h_rs, b_ss, b_rs, ag_ss, ag_rs, gs_sem, gy_ss, gy_rs, gx_ss, gx_rs, ta_sem,
+    part, dg, fl, fr, hs, hr, bs, br, ag, hsb, hrb, bsb, brb, pu, pb, yb, agb, by, s, sb, mask, gh, gmx, gmy, gma,
+    in_sem, out_sem, rs_ss, rs_rs, h_ss, h_rs, b_ss, b_rs, ag_ss, ag_rs,
+    hb_ss, hb_rs, bb_ss, bb_rs, pb_ss, pb_rs, yb_ss, yb_rs, gs_sem, gy_ss, gy_rs, gx_ss, gx_rs, ta_sem,
 ):
     me_x = lax.axis_index("gx")
     me_y = lax.axis_index("gy")
@@ -154,6 +158,20 @@
         to = lax.rem(me_x + d, GX)
         return remote(bs.at[xc, to], br.at[t, xc, me_x], b_ss.at[t, xc, d], b_rs.at[t, xc, d], at_x(d))
 
+    def hb_copy(t, xc, d):
+        to = lax.rem(me_x + d, GX)
+        return remote(hsb.at[xc, to], hrb.at[t, xc, me_x], hb_ss.at[t, xc, d], hb_rs.at[t, xc, d], at_x(d))
+
+    def bb_copy(t, xc, d):
+        to = lax.rem(me_x + d, GX)
+        return remote(bsb.at[xc, to], brb.at[t, xc, me_x], bb_ss.at[t, xc, d], bb_rs.at[t, xc, d], at_x(d))
+
+    def pb_copy(t, rel):
+        return remote(pu.at[2 + rel], pb.at[t, rel], pb_ss.at[t, rel], pb_rs.at[t, rel], at_y(rel))
+
+    def yb_copy(t, rel):
+        return remote(yb.at[t, 0], yb.at[t, GY - rel], yb_ss.at[t, rel], yb_rs.at[t, rel], at_y(rel))
+
     def over_gx(fn):
         def step(d, carry):
             fn(d)
@@ -174,7 +192,16 @@
                 [d[r:r + 64, :128], d[r:r + 64, 128:], d[r + 64:r + 128, :128], d[r + 64:r + 128, 128:]], 0
             )
             o = jnp.dot(a2[...], rhs, preferred_element_type=F32)
-            part[rel, xc, xp * 192:(xp + 1) * 192, :] = o.astype(BF16)
+            part[rel, xc, xp * 128:(xp + 1) * 128, :] = o[:128].astype(BF16)
+            sb[xp * 64:(xp + 1) * 64, :] = o[128:]
+        for gx in range(GX):
+            top = sb[pl.ds(gx, 8, stride=32), :]
+            low = sb[pl.ds(gx + GX, 8, stride=32), :]
+            hsb[xc, gx, rel] = jnp.concatenate([top, low], 0).astype(BF16)
+
+    def send_third(t, xc):
+        over_gx(lambda d: hb_copy(t, xc, d).start())
+        hrb[t, xc, me_x] = hsb[xc, me_x]
 
     def add_part(rel, xc, other):
         part[rel, xc] = (part[rel, xc].astype(F32) + other.astype(F32)).astype(BF16)
@@ -183,10 +210,10 @@
         s[...] = part[0, xc].astype(F32) + fl[t, xc].astype(F32) + fr[t, xc].astype(F32)
 
         def block(gx, carry):
-            for k in range(3):
-                r = gx * 3 + k
-                top = s[pl.ds(r, 8, stride=96), :]
-                low = s[pl.ds(r + KEPT, 8, stride=96), :]
+            for k in range(2):
+                r = gx * 2 + k
+                top = s[pl.ds(r, 8, stride=64), :]
+                low = s[pl.ds(r + 32, 8, stride=64), :]
                 hs[xc, gx, k] = jnp.concatenate([top, low], 0).astype(BF16)
             return carry
 
@@ -194,60 +221,95 @@
         over_gx(lambda d: h_copy(t, xc, d).start())
         hr[t, xc, me_x] = hs[xc, me_x]
 
-    def x_transform(t, put):
-        for k in range(3):
-            hk = hr[t, :, :, k].reshape(512, 128)
-            ht[k * 144:(k + 1) * 144, :] = lax.dot_general(
+    def x_third(t):
+        for rel in range(GY):
+            hk = hrb[t, :, :, rel].reshape(512, 128)
+            ht[rel * 144:(rel + 1) * 144, :] = lax.dot_general(
                 pad[...], hk, NT, preferred_element_type=F32
             ).astype(BF16)
         v = jnp.dot(ht[...], fx[...], preferred_element_type=F32).astype(BF16)
+        pu[2] = v[:144]
+        for rel in (1, 2, 3):
+            pu[2 + rel] = v[rel * 144:(rel + 1) * 144]
+            pb_copy(t, rel).start()
+
+    def x_transform(t, put):
+        for k in range(2):
+            hk = hr[t, :, :, k].reshape(512, 128)
+            v = lax.dot_general(pad[...], hk, NT, preferred_element_type=F32).astype(BF16)
+            pu[k] = jnp.dot(v, fx[...], preferred_element_type=F32).astype(BF16)
+        for rel in (1, 2, 3):
+            pb_copy(t, rel).wait_recv()
+        third = pu[2].astype(F32) + pb[t, 1].astype(F32) + pb[t, 2].astype(F32) + pb[t, 3].astype(F32)
+        v = jnp.concatenate([pu[0], pu[1], third.astype(BF16)], 0)
         for q in range(2):
             for n in range(2):
-                put(q, n * 512, jnp.dot(
-                    v[:, q * 128:(q + 1) * 128], spread[:, n * 512:(n + 1) * 512], preferred_element_type=F32
-                ))
+                put(q, n * 512, jnp.dot(v, spread[q, :, n * 512:(n + 1) * 512], preferred_element_type=F32))
 
     def x_inverse_and_send(t):
-        y = jnp.dot(lw[...], fold[...], preferred_element_type=F32).astype(BF16)
-        for k in range(3):
-            both = jnp.concatenate([y[k * 144:(k + 1) * 144], y[432 + k * 144:432 + (k + 1) * 144]], 1)
-            yk[k] = jnp.dot(padt[...], both, preferred_element_type=F32).astype(BF16)
+        y = jnp.dot(lw[:432, :], fold[0], preferred_element_type=F32)
+        y = (y + jnp.dot(lw[432:, :], fold[1], preferred_element_type=F32)).astype(BF16)
+        for k in (2, 0, 1):
+            v = jnp.dot(padt[...], y[k * 144:(k + 1) * 144], preferred_element_type=F32).astype(BF16)
+            if k == 2:
+                yb[t, 0] = v
+                for rel in (1, 2, 3):
+                    yb_copy(t, rel).start()
+            else:
+                yk[k] = v
         for xc in range(2):
-            for k in range(3):
+            for k in range(2):
                 bx = lax.dot_general(fx[xc * 256:(xc + 1) * 256, :], yk[k], NT, preferred_element_type=F32)
                 bs[xc, :, k] = bx.astype(BF16).reshape(GX, 16, 128)
             over_gx(lambda d: b_copy(t, xc, d).start())
             br[t, xc, me_x] = bs[xc, me_x]
 
+    def third_inverse_and_send(t):
+        for rel in (1, 2, 3):
+            yb_copy(t, rel).wait_recv()
+        for xc in range(2):
+            for rel in range(GY):
+                bx = lax.dot_general(fx[xc * 256:(xc + 1) * 256, :], yb[t, rel], NT, preferred_element_type=F32)
+                bsb[xc, :, rel] = bx.astype(BF16).reshape(GX, 16, 128)
+            over_gx(lambda d: bb_copy(t, xc, d).start())
+            brb[t, xc, me_x] = bsb[xc, me_x]
+
     def gather_block(t, xc):
         over_gx(lambda d: b_copy(t, xc, d).wait_recv())
 
         def block(gx, carry):
-            for k in range(3):
-                r = gx * 3 + k
+            for k in range(2):
+                r = gx * 2 + k
                 v = br[t, xc, gx, k].astype(F32)
-                s[pl.ds(r, 8, stride=96), :] = v[:8]
-                s[pl.ds(r + KEPT, 8, stride=96), :] = v[8:]
+                s[pl.ds(r, 8, stride=64), :] = v[:8]
+                s[pl.ds(r + 32, 8, stride=64), :] = v[8:]
             return carry
 
         lax.fori_loop(0, GX, block, 0)
         ag[t, 0, xc] = s[...].astype(BF16)
 
+    def gather_third(t, xc):
+        over_gx(lambda d: bb_copy(t, xc, d).wait_recv())
+        for rel in range(GY):
+            for gx in range(GX):
+                v = brb[t, xc, gx, rel].astype(F32)
+                sb[pl.ds(gx, 8, stride=32), :] = v[:8]
+                sb[pl.ds(gx + GX, 8, stride=32), :] = v[8:]
+            agb[rel] = sb[...].astype(BF16)
+
     def y_inverse(t, xc):
-        def block(rel, carry):
+        for rel in range(GY):
             h = lax.rem(me_y + rel, GY)
             off = pl.multiple_of(h * 256, 256)
             for xp in range(4):
-                v = jnp.dot(
-                    at2[...], ag[t, rel, xc, xp * 192:(xp + 1) * 192, :], preferred_element_type=F32
-                ).astype(BF16)
+                rhs = jnp.concatenate(
+                    [ag[t, rel, xc, xp * 128:(xp + 1) * 128, :], agb[rel, xp * 64:(xp + 1) * 64, :]], 0
+                )
+                v = jnp.dot(at2[...], rhs, preferred_element_type=F32).astype(BF16)
                 for x2 in range(2):
                     rows = slice(xp * 128 + x2 * 64, xp * 128 + x2 * 64 + 64)
                     by[rows, pl.ds(off, 128)] = v[x2 * 128:x2 * 128 + 64]
                     by[rows, pl.ds(off + 128, 128)] = v[x2 * 128 + 64:x2 * 128 + 128]
-            return carry
-
-        lax.fori_loop(0, GY, block, 0)
 
     def depth_inverse(xc, finish, start=0, stop=5):
         def block(n, carry):
@@ -258,7 +320,7 @@
                 finish(rows, cols, v + lin[rows, cols])
             return carry
 
-        lax.fori_loop(start, stop, block, 0)
+        lax.fori_loop(start, stop, block, 0, unroll=True)
 
     def finish_forward(rows, cols, x):
         k0 = math.sqrt(2.0 / math.pi)
@@ -419,18 +481,19 @@
     forward_block(u, 0, 2)
     pl.semaphore_wait(barrier, 19)
     rs_copy(0, 0).start()
+    loads[4].wait()
+    forward_block(u, 1, 2)
+    rs_copy(0, 3).start()
     loads[3].wait()
     forward_block(u, 0, 3)
     rs_copy(0, 1).start()
-    loads[4].wait()
-    forward_block(u, 1, 2)
-    rs_copy(0, 3).start()
     loads[5].wait()
     forward_block(u, 1, 1)
     rs_copy(0, 4).start()
     forward_block(u, 0, 1)
     loads[6].wait()
     forward_block(u, 0, 0)
+    send_third(0, 0)
     rs_copy(0, 0).wait_recv()
     add_part(1, 0, dg[0, 0])
     rs_copy(0, 2).start()
@@ -439,25 +502,34 @@
     add_part(3, 1, dg[0, 1])
     rs_copy(0, 5).start()
     forward_block(u, 1, 0)
+    send_third(0, 1)
     loads[7].wait()
     fill_weights()
     build_kron((((1,), (0,)), ((), ())))
     for i in range(8, 16):
         loads[i].wait()
-    rs_copy(0, 1).wait_recv()
-    rs_copy(0, 2).wait_recv()
-    sum_and_send(0, 0)
-    rs_copy(0, 4).wait_recv()
-    rs_copy(0, 5).wait_recv()
-    sum_and_send(0, 1)
-    over_gx(lambda d: h_copy(0, 0, d).wait_recv())
-    over_gx(lambda d: h_copy(0, 1, d).wait_recv())
+
+    def sums(t):
+        rs_copy(t, 1).wait_recv()
+        rs_copy(t, 2).wait_recv()
+        sum_and_send(t, 0)
+        rs_copy(t, 4).wait_recv()
+        rs_copy(t, 5).wait_recv()
+        sum_and_send(t, 1)
+        over_gx(lambda d: hb_copy(t, 0, d).wait_recv())
+        over_gx(lambda d: hb_copy(t, 1, d).wait_recv())
+        x_third(t)
+        over_gx(lambda d: h_copy(t, 0, d).wait_recv())
+        over_gx(lambda d: h_copy(t, 1, d).wait_recv())
+
+    sums(0)
 
     x_transform(0, put_uh)
-    lax.fori_loop(0, 3, mix_block, 0)
+    lax.fori_loop(0, 3, mix_block, 0, unroll=True)
     x_inverse_and_send(0)
 
     def gather(t, src):
+        third_inverse_and_send(t)
         gather_block(t, 0)
         ag_copy(t, 0).start()
         ag_copy(t, 1).start()
@@ -477,9 +549,14 @@
     for xc in range(2):
         over_gx(lambda d: h_copy(0, xc, d).wait_send())
         over_gx(lambda d: b_copy(0, xc, d).wait_send())
+        over_gx(lambda d: hb_copy(0, xc, d).wait_send())
+        over_gx(lambda d: bb_copy(0, xc, d).wait_send())
+    for rel in (1, 2, 3):
+        pb_copy(0, rel).wait_send()
 
     ag_copy(0, 1).wait_recv()
     ag_copy(0, 2).wait_recv()
+    gather_third(0, 0)
     y_inverse(0, 0)
     depth_inverse(0, finish_forward)
     act_out = [
@@ -492,8 +569,11 @@
     forward_block(g, 0, 3)
     rs_copy(1, 1).start()
     forward_block(g, 0, 1)
+    forward_block(g, 0, 0)
+    send_third(1, 0)
     ag_copy(0, 4).wait_recv()
     ag_copy(0, 5).wait_recv()
+    gather_third(0, 1)
     y_inverse(0, 1)
     depth_inverse(1, finish_forward, 0, 3)
     rs_copy(1, 0).wait_recv()
@@ -506,29 +586,22 @@
     forward_block(g, 1, 1)
     rs_copy(1, 4).start()
     forward_block(g, 1, 3)
-    forward_block(g, 0, 0)
     forward_block(g, 1, 0)
+    send_third(1, 1)
     rs_copy(1, 3).wait_recv()
     add_part(3, 1, dg[1, 1])
     rs_copy(1, 5).start()
     mixing_terms()
     for rel in (1, 2, 3):
         gy_copy(rel).start()
-    rs_copy(1, 1).wait_recv()
-    rs_copy(1, 2).wait_recv()
-    sum_and_send(1, 0)
-    rs_copy(1, 4).wait_recv()
-    rs_copy(1, 5).wait_recv()
-    sum_and_send(1, 1)
     for rel in (1, 2, 3):
         gy_copy(rel).wait_recv()
     gma[0] = gmy[0] + gmy[1] + gmy[2] + gmy[3]
     over_gx(lambda d: gx_copy(d).start())
-    over_gx(lambda d: h_copy(1, 0, d).wait_recv())
-    over_gx(lambda d: h_copy(1, 1, d).wait_recv())
+    sums(1)
 
     x_transform(1, put_lin)
-    lax.fori_loop(0, 3, adjoint_block, 0)
+    lax.fori_loop(0, 3, adjoint_block, 0, unroll=True)
     x_inverse_and_send(1)
     weight_gradient_send()
     build_kron(TN)
@@ -541,6 +614,7 @@
     act_out[1].wait()
     ag_copy(1, 1).wait_recv()
     ag_copy(1, 2).wait_recv()
+    gather_third(1, 0)
     y_inverse(1, 0)
     depth_inverse(0, finish_backward)
     gf_out = [
@@ -550,6 +624,7 @@
     gf_out[0].start()
     ag_copy(1, 4).wait_recv()
     ag_copy(1, 5).wait_recv()
+    gather_third(1, 1)
     y_inverse(1, 1)
     depth_inverse(1, finish_backward)
     gf_out[1].start()
@@ -566,6 +641,12 @@
     for xc in range(2):
         over_gx(lambda d: h_copy(1, xc, d).wait_send())
         over_gx(lambda d: b_copy(1, xc, d).wait_send())
+        over_gx(lambda d: hb_copy(1, xc, d).wait_send())
+        over_gx(lambda d: bb_copy(1, xc, d).wait_send())
+    for rel in (1, 2, 3):
+        pb_copy(1, rel).wait_send()
+        yb_copy(0, rel).wait_send()
+        yb_copy(1, rel).wait_send()
     gs_copy().wait_send()
     for rel in (1, 2, 3):
         gy_copy(rel).wait_send()
@@ -618,33 +699,42 @@
             vmem((GY * 256, CZ), BF16),
             vmem((CZ, CZ), BF16),
             vmem((ROWS, CZ), F32),
-            vmem((512, 256), BF16),
+            vmem((512, 128), BF16),
             vmem((144, 128), BF16),
             vmem((128, 144), BF16),
-            vmem((128, 1024), BF16),
-            vmem((1024, 128), BF16),
+            vmem((2, 128, 1024), BF16),
+            vmem((2, 1024, 128), BF16),
             vmem((192, 256), BF16),
             vmem((256, 192), BF16),
             vmem((3, 6, C, 2, C * KEPT), BF16),
             vmem((C, CZ), F32),
             vmem((3, 6, 2, 24, 1024), F32),
             vmem((2, 432, 1024), F32),
-            vmem((432, 512), BF16),
-            vmem((3, 128, 256), BF16),
+            vmem((576, 512), BF16),
+            vmem((2, 128, 128), BF16),
             vmem((864, 1024), BF16),
             vmem((432, 1024), BF16),
             vmem((432, 1024), BF16),
-            vmem((4, 2, 768, 128), BF16),
-            vmem((2, 2, 768, 128), BF16),
-            vmem((2, 2, 768, 128), BF16),
-            vmem((2, 2, 768, 128), BF16),
-            vmem((2, GX, 3, 16, 128), BF16),
-            vmem((2, 2, GX, 3, 16, 128), BF16),
-            vmem((2, GX, 3, 16, 128), BF16),
-            vmem((2, 2, GX, 3, 16, 128), BF16),
-            vmem((2, 4, 2, 768, 128), BF16),
+            vmem((4, 2, 512, 128), BF16),
+            vmem((2, 2, 512, 128), BF16),
+            vmem((2, 2, 512, 128), BF16),
+            vmem((2, 2, 512, 128), BF16),
+            vmem((2, GX, 2, 16, 128), BF16),
+            vmem((2, 2, GX, 2, 16, 128), BF16),
+            vmem((2, GX, 2, 16, 128), BF16),
+            vmem((2, 2, GX, 2, 16, 128), BF16),
+            vmem((2, 4, 2, 512, 128), BF16),
+            vmem((2, GX, GY, 16, 128), BF16),
+            vmem((2, 2, GX, GY, 16, 128), BF16),
+            vmem((2, GX, GY, 16, 128), BF16),
+            vmem((2, 2, GX, GY, 16, 128), BF16),
+            vmem((6, 144, 128), BF16),
+            vmem((2, GY, 144, 128), BF16),
+            vmem((2, GY, 128, 128), BF16),
+            vmem((GY, 256, 128), BF16),
             vmem((HALF, 1024), BF16),
-            vmem((768, 128), F32),
+            vmem((512, 128), F32),
+            vmem((256, 128), F32),
             vmem((24, 1024), F32),
             vmem((3, 6, 8, 1024), F32),
             vmem((5, 8, CZ), F32),
@@ -660,6 +750,14 @@
             dma((2, 2, GX)),
             dma((2, 6)),
             dma((2, 6)),
+            dma((2, 2, GX)),
+            dma((2, 2, GX)),
+            dma((2, 2, GX)),
+            dma((2, 2, GX)),
+            dma((2, GY)),
+            dma((2, GY)),
+            dma((2, GY)),
+            dma((2, GY)),
             dma((2,)),
             dma((4,)),
             dma((4,)),

time: 126 us -> 119 us (0.944)
  Pallas kernels: 124 us -> 118 us
    pallas_call x1, Pallas kernels: 118 us -> 112 us  [shards(): pl.pallas_call(kernel, out_shape=results, in_specs=[hbm, hbm, hbm, local]...]
where the time goes in v2:
time: 119 us
  Pallas kernels  118 us (99%)
    pallas_call x1, Pallas kernels, shards(): pl.pallas_call(kernel, out_shape=results, in_specs=[hbm, hbm, hbm, local]...  112 us
    pallas_call x1, Pallas kernels, shards(): pl.pallas_call(hand_over, out_shape=results, in_specs=[hbm] * 4, out_spec...  5.69 us

profile of v2, /device:TPU:0, one launch (start us, length us, event | category | flops | bytes accessed | tf_op | source)
XLA Modules:
  0.0 118.6 jit_solution(21042188757409303)
XLA Ops:
  0.6 112.1 %shard_map.156 = (bf16[1024,1280]{1,0:T(8,128)(2,1)}, bf16[1024,1280]{1,0:T(8,128)(2,1)}, f32[3,3,20,2,960]{4,3,2,1,0:T(2,128)}, f32[20,20]{1,0:T(8,128)}) custom-call(bf16[1024,1280]{1,0:T(8,128)(2,1)} %bitcast.6, bf16[1024,1280]{1,0:T(8,128)(2,1)} %bitcast.7, bf16[3,6,20,2,960]{4,3,2,1,0:T(2,128)(2,1)} %bitcast.8, bf16[20,20]{1,0:T(8,128)(2,1)} %mix_ref.1, ...), custom_call_target="tpu_custom_call" | custom-call | tf_op jit(solution)/shard_map/pallas_call | solution.py:688
  112.8 5.7 %shard_map.157 = (bf16[1024,1280]{1,0:T(8,128)(2,1)}, bf16[1024,1280]{1,0:T(8,128)(2,1)}, f32[3,3,20,2,960]{4,3,2,1,0:T(2,128)}, f32[20,20]{1,0:T(8,128)}) custom-call(bf16[1024,1280]{1,0:T(8,128)(2,1)} %get-tuple-element.12.act_in, bf16[1024,1280]{1,0:T(8,128)(2,1)} %get-tuple-element.13.gf_in, f32[3,3,20,2,960]{4,3,2,1,0:T(2,128)} %get-tuple-element.14.gs_in, ...), custom_call_target="tpu_custom_call" | custom-call | tf_op jit(solution)/shard_map/pallas_call | solution.py:775

commit v3 on v2

--- a/solution.py
+++ b/solution.py
@@ -103,14 +103,23 @@
     loads = [
         pltpu.make_async_copy(src, dst, in_sem.at[i])
         for i, (src, dst) in enumerate([
-            (u_hbm.at[first], u.at[first]), (ee_hbm.at[opposite], ee.at[opposite]), (a2_hbm.at[me_y], a2),
-            (ee_hbm.at[left], ee.at[left]), (u_hbm.at[second], u.at[second]), (ee_hbm.at[right], ee.at[right]),
-            (ee_hbm.at[me_y], ee.at[me_y]), (w_hbm, w), (fx_hbm, fx), (pad_hbm, pad), (padt_hbm, padt),
+            (u_hbm.at[first], u.at[first]), (ee_hbm.at[opposite], ee.at[opposite]),
+            (ee_hbm.at[right], ee.at[right]), (a2_hbm.at[me_y], a2),
+            (ee_hbm.at[left], ee.at[left]), (ee_hbm.at[me_y], ee.at[me_y]), (u_hbm.at[second], u.at[second]),
+            (w_hbm, w), (fx_hbm, fx), (pad_hbm, pad), (padt_hbm, padt),
             (spread_hbm, spread), (fold_hbm, fold), (at2_hbm.at[me_y], at2), (eet_hbm, eet), (cot_hbm, cot),
         ])
     ]
-    for load in loads:
-        load.start()
+
+    def start_loads(*ids):
+        for i in ids:
+            loads[i].start()
+
+    def wait_loads(*ids):
+        for i in ids:
+            loads[i].wait()
+
+    start_loads(0, 1, 2, 3)
 
     barrier = pltpu.get_barrier_semaphore()
     for rel in (1, 2, 3):
@@ -128,27 +137,29 @@
             src_ref=src, dst_ref=dst, send_sem=ss, recv_sem=rs, device_id=dev, device_id_type=MESH
         )
 
-    def rs_copy(t, i):
+    upper, lower = pl.ds(0, 256), pl.ds(256, 256)
+
+    def rs_copy(t, c, i):
         src, dst, rel = [
-            (part.at[2, 0], dg.at[t, 0], 1),
-            (part.at[3, 0], fr.at[t, 0], 3),
-            (part.at[1, 0], fl.at[t, 0], 1),
-            (part.at[2, 1], dg.at[t, 1], 3),
-            (part.at[1, 1], fl.at[t, 1], 1),
-            (part.at[3, 1], fr.at[t, 1], 3),
+            (part.at[2, c, upper], dg.at[t, c, upper], 1),
+            (part.at[2, c, lower], dg.at[t, c, lower], 3),
+            (part.at[1, c, lower], fl.at[t, c, lower], 1),
+            (part.at[3, c, upper], fr.at[t, c, upper], 3),
+            (part.at[1, c, upper], fl.at[t, c, upper], 1),
+            (part.at[3, c, lower], fr.at[t, c, lower], 3),
         ][i]
-        return remote(src, dst, rs_ss.at[t, i], rs_rs.at[t, i], at_y(rel))
-
-    def ag_copy(t, i):
+        return remote(src, dst, rs_ss.at[t, c, i], rs_rs.at[t, c, i], at_y(rel))
+
+    def ag_copy(t, c, i):
         src, dst, rel = [
-            (ag.at[t, 0, 0], ag.at[t, 3, 0], 1),
-            (ag.at[t, 0, 0], ag.at[t, 1, 0], 3),
-            (ag.at[t, 3, 0], ag.at[t, 2, 0], 1),
-            (ag.at[t, 0, 1], ag.at[t, 1, 1], 3),
-            (ag.at[t, 0, 1], ag.at[t, 3, 1], 1),
-            (ag.at[t, 1, 1], ag.at[t, 2, 1], 3),
+            (ag.at[t, 0, c, upper], ag.at[t, 3, c, upper], 1),
+            (ag.at[t, 0, c, lower], ag.at[t, 1, c, lower], 3),
+            (ag.at[t, 0, c, lower], ag.at[t, 3, c, lower], 1),
+            (ag.at[t, 0, c, upper], ag.at[t, 1, c, upper], 3),
+            (ag.at[t, 3, c, upper], ag.at[t, 2, c, upper], 1),
+            (ag.at[t, 1, c, lower], ag.at[t, 2, c, lower], 3),
         ][i]
-        return remote(src, dst, ag_ss.at[t, i], ag_rs.at[t, i], at_y(rel))
+        return remote(src, dst, ag_ss.at[t, c, i], ag_rs.at[t, c, i], at_y(rel))
 
     def h_copy(t, xc, d):
         to = lax.rem(me_x + d, GX)
@@ -183,28 +194,54 @@
         first = (me_y == 0) & (jl == 0)
         return jnp.where(first, 1.0, 2.0).astype(F32) * (1.0 / float(NX * NY * NZ))
 
-    def forward_block(src, xc, rel):
-        h = lax.rem(me_y + rel, GY)
-        d = jnp.dot(src[xc * HALF:(xc + 1) * HALF, :], ee[h], preferred_element_type=F32).astype(BF16)
-        for xp in range(4):
-            r = xp * 128
-            rhs = jnp.concatenate(
-                [d[r:r + 64, :128], d[r:r + 64, 128:], d[r + 64:r + 128, :128], d[r + 64:r + 128, 128:]], 0
-            )
-            o = jnp.dot(a2[...], rhs, preferred_element_type=F32)
-            part[rel, xc, xp * 128:(xp + 1) * 128, :] = o[:128].astype(BF16)
-            sb[xp * 64:(xp + 1) * 64, :] = o[128:]
-        for gx in range(GX):
-            top = sb[pl.ds(gx, 8, stride=32), :]
-            low = sb[pl.ds(gx + GX, 8, stride=32), :]
-            hsb[xc, gx, rel] = jnp.concatenate([top, low], 0).astype(BF16)
+    def forward_block(src, xc, *rels):
+        tab = [ee[lax.rem(me_y + rel, GY)] for rel in rels]
+        tab = tab[0] if len(tab) == 1 else jnp.concatenate(tab, 1)
+        both = jnp.dot(src[xc * HALF:(xc + 1) * HALF, :], tab, preferred_element_type=F32).astype(BF16)
+        for i, rel in enumerate(rels):
+            d = both[:, i * 256:(i + 1) * 256]
+            for xp in range(4):
+                r = xp * 128
+                rhs = jnp.concatenate(
+                    [d[r:r + 64, :128], d[r:r + 64, 128:], d[r + 64:r + 128, :128], d[r + 64:r + 128, 128:]], 0
+                )
+                o = jnp.dot(a2[...], rhs, preferred_element_type=F32)
+                part[rel, xc, xp * 128:(xp + 1) * 128, :] = o[:128].astype(BF16)
+                sb[i, xp * 64:(xp + 1) * 64, :] = o[128:]
+        for i, rel in enumerate(rels):
+            for gx in range(GX):
+                top = sb[i, pl.ds(gx, 8, stride=32), :]
+                low = sb[i, pl.ds(gx + GX, 8, stride=32), :]
+                hsb[xc, gx, rel] = jnp.concatenate([top, low], 0).astype(BF16)
 
     def send_third(t, xc):
         over_gx(lambda d: hb_copy(t, xc, d).start())
         hrb[t, xc, me_x] = hsb[xc, me_x]
 
-    def add_part(rel, xc, other):
-        part[rel, xc] = (part[rel, xc].astype(F32) + other.astype(F32)).astype(BF16)
+    def rs_start(t, c, *ids):
+        for i in ids:
+            rs_copy(t, c, i).start()
+
+    def rs_forward(t, c):
+        rs_copy(t, c, 0).wait_recv()
+        part[1, c, :256] = (part[1, c, :256].astype(F32) + dg[t, c, :256].astype(F32)).astype(BF16)
+        rs_start(t, c, 4)
+        rs_copy(t, c, 1).wait_recv()
+        part[3, c, 256:] = (part[3, c, 256:].astype(F32) + dg[t, c, 256:].astype(F32)).astype(BF16)
+        rs_start(t, c, 5)
+
+    def ag_start(t, c):
+        for i in range(4):
+            ag_copy(t, c, i).start()
+
+    def ag_forward(t, c):
+        for i in (0, 1):
+            ag_copy(t, c, i).wait_recv()
+            ag_copy(t, c, 4 + i).start()
+
+    def ag_finish(t, c):
+        for i in (2, 3, 4, 5):
+            ag_copy(t, c, i).wait_recv()
 
     def sum_and_send(t, xc):
         s[...] = part[0, xc].astype(F32) + fl[t, xc].astype(F32) + fr[t, xc].astype(F32)
@@ -293,9 +330,9 @@
         for rel in range(GY):
             for gx in range(GX):
                 v = brb[t, xc, gx, rel].astype(F32)
-                sb[pl.ds(gx, 8, stride=32), :] = v[:8]
-                sb[pl.ds(gx + GX, 8, stride=32), :] = v[8:]
-            agb[rel] = sb[...].astype(BF16)
+                sb[rel, pl.ds(gx, 8, stride=32), :] = v[:8]
+                sb[rel, pl.ds(gx + GX, 8, stride=32), :] = v[8:]
+            agb[rel] = sb[rel].astype(BF16)
 
     def y_inverse(t, xc):
         for rel in range(GY):
@@ -356,7 +393,7 @@
             lin[rows, cols] = jnp.dot(src[rows, :], kron[:, cols], preferred_element_type=F32)
             return carry
 
-        lax.fori_loop(0, 5, block, 0)
+        lax.fori_loop(0, 5, block, 0, unroll=True)
 
     def fill_weights():
         wp[...] = jnp.zeros_like(wp)
@@ -476,53 +513,42 @@
     def ta_copy():
         return remote(gma.at[16], gma.at[17], ta_sem.at[0], ta_sem.at[1], twin)
 
-    for i in range(3):
-        loads[i].wait()
-    forward_block(u, 0, 2)
+    wait_loads(0, 1, 2, 3)
+    start_loads(4, 5, 6)
+    forward_block(u, 0, 2, 1)
     pl.semaphore_wait(barrier, 19)
-    rs_copy(0, 0).start()
-    loads[4].wait()
-    forward_block(u, 1, 2)
-    rs_copy(0, 3).start()
-    loads[3].wait()
-    forward_block(u, 0, 3)
-    rs_copy(0, 1).start()
-    loads[5].wait()
-    forward_block(u, 1, 1)
-    rs_copy(0, 4).start()
-    forward_block(u, 0, 1)
-    loads[6].wait()
-    forward_block(u, 0, 0)
+    rs_start(0, 0, 0, 1, 2)
+    wait_loads(4, 5)
+    forward_block(u, 0, 3, 0)
+    rs_start(0, 0, 3)
     send_third(0, 0)
-    rs_copy(0, 0).wait_recv()
-    add_part(1, 0, dg[0, 0])
-    rs_copy(0, 2).start()
-    forward_block(u, 1, 3)
-    rs_copy(0, 3).wait_recv()
-    add_part(3, 1, dg[0, 1])
-    rs_copy(0, 5).start()
-    forward_block(u, 1, 0)
+    wait_loads(6)
+    start_loads(*range(7, 16))
+    forward_block(u, 1, 2, 1)
+    rs_start(0, 1, 0, 1)
+    forward_block(u, 1, 3, 0)
     send_third(0, 1)
-    loads[7].wait()
+    rs_forward(0, 0)
+    rs_start(0, 1, 2, 3)
+    wait_loads(7)
     fill_weights()
+    rs_forward(0, 1)
     build_kron((((1,), (0,)), ((), ())))
-    for i in range(8, 16):
-        loads[i].wait()
-
-    def sums(t):
-        rs_copy(t, 1).wait_recv()
-        rs_copy(t, 2).wait_recv()
-        sum_and_send(t, 0)
-        rs_copy(t, 4).wait_recv()
-        rs_copy(t, 5).wait_recv()
-        sum_and_send(t, 1)
+    wait_loads(*range(8, 16))
+
+    def sums(t, meanwhile):
+        for c in range(2):
+            for i in (2, 3, 4, 5):
+                rs_copy(t, c, i).wait_recv()
+            sum_and_send(t, c)
+        meanwhile()
         over_gx(lambda d: hb_copy(t, 0, d).wait_recv())
         over_gx(lambda d: hb_copy(t, 1, d).wait_recv())
         x_third(t)
         over_gx(lambda d: h_copy(t, 0, d).wait_recv())
         over_gx(lambda d: h_copy(t, 1, d).wait_recv())
 
-    sums(0)
+    sums(0, lambda: None)
 
     x_transform(0, put_uh)
     lax.fori_loop(0, 3, mix_block, 0, unroll=True)
@@ -531,21 +557,18 @@
     def gather(t, src):
         third_inverse_and_send(t)
         gather_block(t, 0)
-        ag_copy(t, 0).start()
-        ag_copy(t, 1).start()
+        ag_start(t, 0)
         gather_block(t, 1)
-        ag_copy(t, 3).start()
         linear(src, 0)
-        ag_copy(t, 0).wait_recv()
-        ag_copy(t, 2).start()
-        ag_copy(t, 4).start()
-        ag_copy(t, 3).wait_recv()
-        ag_copy(t, 5).start()
+        ag_forward(t, 0)
+        ag_start(t, 1)
         linear(src, 1)
+        ag_forward(t, 1)
 
     gather(0, u)
     for i in range(6):
-        rs_copy(0, i).wait_send()
+        rs_copy(0, 0, i).wait_send()
+        rs_copy(0, 1, i).wait_send()
     for xc in range(2):
         over_gx(lambda d: h_copy(0, xc, d).wait_send())
         over_gx(lambda d: b_copy(0, xc, d).wait_send())
@@ -554,8 +577,7 @@
     for rel in (1, 2, 3):
         pb_copy(0, rel).wait_send()
 
-    ag_copy(0, 1).wait_recv()
-    ag_copy(0, 2).wait_recv()
+    ag_finish(0, 0)
     gather_third(0, 0)
     y_inverse(0, 0)
     depth_inverse(0, finish_forward)
@@ -564,46 +586,40 @@
         for xc in range(2)
     ]
     act_out[0].start()
-    forward_block(g, 0, 2)
-    rs_copy(1, 0).start()
-    forward_block(g, 0, 3)
-    rs_copy(1, 1).start()
-    forward_block(g, 0, 1)
-    forward_block(g, 0, 0)
+    forward_block(g, 0, 2, 1)
+    rs_start(1, 0, 0, 1, 2)
+    forward_block(g, 0, 3, 0)
+    rs_start(1, 0, 3)
     send_third(1, 0)
-    ag_copy(0, 4).wait_recv()
-    ag_copy(0, 5).wait_recv()
+    ag_finish(0, 1)
     gather_third(0, 1)
     y_inverse(0, 1)
     depth_inverse(1, finish_forward, 0, 3)
-    rs_copy(1, 0).wait_recv()
-    add_part(1, 0, dg[1, 0])
-    rs_copy(1, 2).start()
+    rs_forward(1, 0)
     depth_inverse(1, finish_forward, 3, 5)
     act_out[1].start()
-    forward_block(g, 1, 2)
-    rs_copy(1, 3).start()
-    forward_block(g, 1, 1)
-    rs_copy(1, 4).start()
-    forward_block(g, 1, 3)
-    forward_block(g, 1, 0)
+    forward_block(g, 1, 2, 1)
+    rs_start(1, 1, 0, 1, 2)
+    forward_block(g, 1, 3, 0)
+    rs_start(1, 1, 3)
     send_third(1, 1)
-    rs_copy(1, 3).wait_recv()
-    add_part(3, 1, dg[1, 1])
-    rs_copy(1, 5).start()
-    mixing_terms()
-    for rel in (1, 2, 3):
-        gy_copy(rel).start()
+    rs_forward(1, 1)
+
+    def mixing_send():
+        mixing_terms()
+        for rel in (1, 2, 3):
+            gy_copy(rel).start()
+
+    sums(1, mixing_send)
+
+    x_transform(1, put_lin)
+    lax.fori_loop(0, 3, adjoint_block, 0, unroll=True)
+    x_inverse_and_send(1)
+    weight_gradient_send()
     for rel in (1, 2, 3):
         gy_copy(rel).wait_recv()
     gma[0] = gmy[0] + gmy[1] + gmy[2] + gmy[3]
     over_gx(lambda d: gx_copy(d).start())
-    sums(1)
-
-    x_transform(1, put_lin)
-    lax.fori_loop(0, 3, adjoint_block, 0, unroll=True)
-    x_inverse_and_send(1)
-    weight_gradient_send()
     build_kron(TN)
     gather(1, g)
     over_gx(lambda d: gx_copy(d).wait_recv())
@@ -612,8 +628,7 @@
     weight_gradient_finish()
     act_out[0].wait()
     act_out[1].wait()
-    ag_copy(1, 1).wait_recv()
-    ag_copy(1, 2).wait_recv()
+    ag_finish(1, 0)
     gather_third(1, 0)
     y_inverse(1, 0)
     depth_inverse(0, finish_backward)
@@ -622,8 +637,7 @@
         for xc in range(2)
     ]
     gf_out[0].start()
-    ag_copy(1, 4).wait_recv()
-    ag_copy(1, 5).wait_recv()
+    ag_finish(1, 1)
     gather_third(1, 1)
     y_inverse(1, 1)
     depth_inverse(1, finish_backward)
@@ -633,11 +647,11 @@
     for cb in range(5):
         gm_ref[cb * 4:(cb + 1) * 4, :] = total[cb * 8:cb * 8 + 4, :C]
 
-    for t in range(2):
-        for i in range(6):
-            ag_copy(t, i).wait_send()
     for i in range(6):
-        rs_copy(1, i).wait_send()
+        for c in range(2):
+            ag_copy(0, c, i).wait_send()
+            ag_copy(1, c, i).wait_send()
+            rs_copy(1, c, i).wait_send()
     for xc in range(2):
         over_gx(lambda d: h_copy(1, xc, d).wait_send())
         over_gx(lambda d: b_copy(1, xc, d).wait_send())
@@ -734,7 +748,7 @@
             vmem((GY, 256, 128), BF16),
             vmem((HALF, 1024), BF16),
             vmem((512, 128), F32),
-            vmem((256, 128), F32),
+            vmem((GY, 256, 128), F32),
             vmem((24, 1024), F32),
             vmem((3, 6, 8, 1024), F32),
             vmem((5, 8, CZ), F32),
@@ -742,14 +756,14 @@
             vmem((18, 40, 128), F32),
             dma((16,)),
             dma((2, 2)),
-            dma((2, 6)),
-            dma((2, 6)),
+            dma((2, 2, 6)),
+            dma((2, 2, 6)),
             dma((2, 2, GX)),
             dma((2, 2, GX)),
             dma((2, 2, GX)),
             dma((2, 2, GX)),
-            dma((2, 6)),
-            dma((2, 6)),
+            dma((2, 2, 6)),
+            dma((2, 2, 6)),
             dma((2, 2, GX)),
             dma((2, 2, GX)),
             dma((2, 2, GX)),

time: 119 us -> 111 us (0.933)
  Pallas kernels: 118 us -> 110 us
    pallas_call x1, Pallas kernels: 112 us -> 104 us  [shards(): pl.pallas_call(kernel, out_shape=results, in_specs=[hbm, hbm, hbm, local]...]
where the time goes in v3:
time: 111 us
  Pallas kernels  110 us (99%)
    pallas_call x1, Pallas kernels, shards(): pl.pallas_call(kernel, out_shape=results, in_specs=[hbm, hbm, hbm, local]...  104 us
    pallas_call x1, Pallas kernels, shards(): pl.pallas_call(hand_over, out_shape=results, in_specs=[hbm] * 4, out_spec...  5.69 us

profile of v3, /device:TPU:0, one launch (start us, length us, event | category | flops | bytes accessed | tf_op | source)
XLA Modules:
  0.0 110.7 jit_solution(17528980028390038799)
XLA Ops:
  0.6 104.2 %shard_map.156 = (bf16[1024,1280]{1,0:T(8,128)(2,1)}, bf16[1024,1280]{1,0:T(8,128)(2,1)}, f32[3,3,20,2,960]{4,3,2,1,0:T(2,128)}, f32[20,20]{1,0:T(8,128)}) custom-call(bf16[1024,1280]{1,0:T(8,128)(2,1)} %bitcast.6, bf16[1024,1280]{1,0:T(8,128)(2,1)} %bitcast.7, bf16[3,6,20,2,960]{4,3,2,1,0:T(2,128)(2,1)} %bitcast.8, bf16[20,20]{1,0:T(8,128)(2,1)} %mix_ref.1, ...), custom_call_target="tpu_custom_call" | custom-call | tf_op jit(solution)/shard_map/pallas_call | solution.py:702
  104.9 5.7 %shard_map.157 = (bf16[1024,1280]{1,0:T(8,128)(2,1)}, bf16[1024,1280]{1,0:T(8,128)(2,1)}, f32[3,3,20,2,960]{4,3,2,1,0:T(2,128)}, f32[20,20]{1,0:T(8,128)}) custom-call(bf16[1024,1280]{1,0:T(8,128)(2,1)} %get-tuple-element.12.act_in, bf16[1024,1280]{1,0:T(8,128)(2,1)} %get-tuple-element.13.gf_in, f32[3,3,20,2,960]{4,3,2,1,0:T(2,128)} %get-tuple-element.14.gs_in, ...), custom_call_target="tpu_custom_call" | custom-call | tf_op jit(solution)/shard_map/pallas_call | solution.py:789

commit v4 on v3

--- a/solution.py
+++ b/solution.py
@@ -82,8 +82,7 @@
     act_hbm, gf_hbm, gs_ref, gm_ref,
     u, cot, g, out, ee, eet, kron, lin, fx, pad, padt, spread, fold, a2, at2, w, mixrows, wp, uh, ht, yk, lw, gss, gsr,
     part, dg, fl, fr, hs, hr, bs, br, ag, hsb, hrb, bsb, brb, pu, pb, yb, agb, by, s, sb, mask, gh, gmx, gmy, gma,
-    in_sem, out_sem, rs_ss, rs_rs, h_ss, h_rs, b_ss, b_rs, ag_ss, ag_rs,
-    hb_ss, hb_rs, bb_ss, bb_rs, pb_ss, pb_rs, yb_ss, yb_rs, gs_sem, gy_ss, gy_rs, gx_ss, gx_rs, ta_sem,
+    in_sem, out_sem, rs_ss, rs_rs, ag_ss, ag_rs, ex_ss, ex_rs, third_ss, third_rs, gs_sem, gm_ss, gm_rs, ta_sem,
 ):
     me_x = lax.axis_index("gx")
     me_y = lax.axis_index("gy")
@@ -148,7 +147,7 @@
             (part.at[1, c, upper], fl.at[t, c, upper], 1),
             (part.at[3, c, lower], fr.at[t, c, lower], 3),
         ][i]
-        return remote(src, dst, rs_ss.at[t, c, i], rs_rs.at[t, c, i], at_y(rel))
+        return remote(src, dst, rs_ss.at[t], rs_rs.at[t, c, min(i, 2)], at_y(rel))
 
     def ag_copy(t, c, i):
         src, dst, rel = [
@@ -159,29 +158,59 @@
             (ag.at[t, 3, c, upper], ag.at[t, 2, c, upper], 1),
             (ag.at[t, 1, c, lower], ag.at[t, 2, c, lower], 3),
         ][i]
-        return remote(src, dst, ag_ss.at[t, c, i], ag_rs.at[t, c, i], at_y(rel))
-
-    def h_copy(t, xc, d):
-        to = lax.rem(me_x + d, GX)
-        return remote(hs.at[xc, to], hr.at[t, xc, me_x], h_ss.at[t, xc, d], h_rs.at[t, xc, d], at_x(d))
-
-    def b_copy(t, xc, d):
-        to = lax.rem(me_x + d, GX)
-        return remote(bs.at[xc, to], br.at[t, xc, me_x], b_ss.at[t, xc, d], b_rs.at[t, xc, d], at_x(d))
-
-    def hb_copy(t, xc, d):
-        to = lax.rem(me_x + d, GX)
-        return remote(hsb.at[xc, to], hrb.at[t, xc, me_x], hb_ss.at[t, xc, d], hb_rs.at[t, xc, d], at_x(d))
-
-    def bb_copy(t, xc, d):
-        to = lax.rem(me_x + d, GX)
-        return remote(bsb.at[xc, to], brb.at[t, xc, me_x], bb_ss.at[t, xc, d], bb_rs.at[t, xc, d], at_x(d))
+        return remote(src, dst, ag_ss.at[t], ag_rs.at[t, c, min(i, 2)], at_y(rel))
+
+    def rs_rest(t, c):
+        remote(part.at[0], fl.at[t], rs_ss.at[t], rs_rs.at[t, c, 2], at_y(1)).wait_recv()
+
+    def rs_sent(t):
+        remote(part.at[pl.ds(0, 3)], part.at[pl.ds(0, 3)], rs_ss.at[t], rs_rs.at[t, 0, 2], at_y(1)).wait_send()
+
+    def ag_sent(t):
+        blocks = ag.at[t, pl.ds(0, 3)]
+        remote(blocks, blocks, ag_ss.at[t], ag_rs.at[t, 0, 2], at_y(1)).wait_send()
+
+    H, B, HB, BB = range(4)
+    pairs = ((hs, hr), (bs, br), (hsb, hrb), (bsb, brb))
+    others = pl.ds(0, GX - 1)
+
+    def exchange(kind, t, xc):
+        src, dst = pairs[kind]
+
+        def step(d, carry):
+            to = lax.rem(me_x + d, GX)
+            remote(
+                src.at[xc, to], dst.at[t, xc, me_x], ex_ss.at[kind, t], ex_rs.at[kind, t, xc], at_x(d)
+            ).start()
+            return carry
+
+        lax.fori_loop(1, GX, step, 0)
+        dst[t, xc, me_x] = src[xc, me_x]
+
+    def arrived(kind, t, xc):
+        src, dst = pairs[kind]
+        remote(
+            src.at[xc, others], dst.at[t, xc, others], ex_ss.at[kind, t], ex_rs.at[kind, t, xc], at_x(1)
+        ).wait_recv()
+
+    def departed(kind, t):
+        src, dst = pairs[kind]
+        remote(
+            src.at[:, others], dst.at[t, :, others], ex_ss.at[kind, t], ex_rs.at[kind, t, 0], at_x(1)
+        ).wait_send()
 
     def pb_copy(t, rel):
-        return remote(pu.at[2 + rel], pb.at[t, rel], pb_ss.at[t, rel], pb_rs.at[t, rel], at_y(rel))
+        return remote(pu.at[2 + rel], pb.at[t, rel], third_ss.at[t, 0], third_rs.at[t, 0], at_y(rel))
 
     def yb_copy(t, rel):
-        return remote(yb.at[t, 0], yb.at[t, GY - rel], yb_ss.at[t, rel], yb_rs.at[t, rel], at_y(rel))
+        return remote(yb.at[t, 0], yb.at[t, GY - rel], third_ss.at[t, 1], third_rs.at[t, 1], at_y(rel))
+
+    def pb_all(t):
+        return remote(pu.at[pl.ds(0, 3)], pb.at[t, pl.ds(0, 3)], third_ss.at[t, 0], third_rs.at[t, 0], at_y(1))
+
+    def yb_all(t):
+        blocks = yb.at[t, pl.ds(0, 3)]
+        return remote(blocks, blocks, third_ss.at[t, 1], third_rs.at[t, 1], at_y(1))
 
     def over_gx(fn):
         def step(d, carry):
@@ -215,8 +244,7 @@
                 hsb[xc, gx, rel] = jnp.concatenate([top, low], 0).astype(BF16)
 
     def send_third(t, xc):
-        over_gx(lambda d: hb_copy(t, xc, d).start())
-        hrb[t, xc, me_x] = hsb[xc, me_x]
+        exchange(HB, t, xc)
 
     def rs_start(t, c, *ids):
         for i in ids:
@@ -240,8 +268,7 @@
             ag_copy(t, c, 4 + i).start()
 
     def ag_finish(t, c):
-        for i in (2, 3, 4, 5):
-            ag_copy(t, c, i).wait_recv()
+        remote(ag.at[t, 0], ag.at[t, 0], ag_ss.at[t], ag_rs.at[t, c, 2], at_y(1)).wait_recv()
 
     def sum_and_send(t, xc):
         s[...] = part[0, xc].astype(F32) + fl[t, xc].astype(F32) + fr[t, xc].astype(F32)
@@ -255,8 +282,7 @@
             return carry
 
         lax.fori_loop(0, GX, block, 0)
-        over_gx(lambda d: h_copy(t, xc, d).start())
-        hr[t, xc, me_x] = hs[xc, me_x]
+        exchange(H, t, xc)
 
     def x_third(t):
         for rel in range(GY):
@@ -275,8 +301,7 @@
             hk = hr[t, :, :, k].reshape(512, 128)
             v = lax.dot_general(pad[...], hk, NT, preferred_element_type=F32).astype(BF16)
             pu[k] = jnp.dot(v, fx[...], preferred_element_type=F32).astype(BF16)
-        for rel in (1, 2, 3):
-            pb_copy(t, rel).wait_recv()
+        pb_all(t).wait_recv()
         third = pu[2].astype(F32) + pb[t, 1].astype(F32) + pb[t, 2].astype(F32) + pb[t, 3].astype(F32)
         v = jnp.concatenate([pu[0], pu[1], third.astype(BF16)], 0)
         for q in range(2):
@@ -298,21 +323,18 @@
             for k in range(2):
                 bx = lax.dot_general(fx[xc * 256:(xc + 1) * 256, :], yk[k], NT, preferred_element_type=F32)
                 bs[xc, :, k] = bx.astype(BF16).reshape(GX, 16, 128)
-            over_gx(lambda d: b_copy(t, xc, d).start())
-            br[t, xc, me_x] = bs[xc, me_x]
+            exchange(B, t, xc)
 
     def third_inverse_and_send(t):
-        for rel in (1, 2, 3):
-            yb_copy(t, rel).wait_recv()
+        yb_all(t).wait_recv()
         for xc in range(2):
             for rel in range(GY):
                 bx = lax.dot_general(fx[xc * 256:(xc + 1) * 256, :], yb[t, rel], NT, preferred_element_type=F32)
                 bsb[xc, :, rel] = bx.astype(BF16).reshape(GX, 16, 128)
-            over_gx(lambda d: bb_copy(t, xc, d).start())
-            brb[t, xc, me_x] = bsb[xc, me_x]
+            exchange(BB, t, xc)
 
     def gather_block(t, xc):
-        over_gx(lambda d: b_copy(t, xc, d).wait_recv())
+        arrived(B, t, xc)
 
         def block(gx, carry):
             for k in range(2):
@@ -326,7 +348,7 @@
         ag[t, 0, xc] = s[...].astype(BF16)
 
     def gather_third(t, xc):
-        over_gx(lambda d: bb_copy(t, xc, d).wait_recv())
+        arrived(BB, t, xc)
         for rel in range(GY):
             for gx in range(GX):
                 v = brb[t, xc, gx, rel].astype(F32)
@@ -505,10 +527,16 @@
         gmy[0] = jnp.dot(hi, sel, preferred_element_type=F32) + jnp.dot(low, sel, preferred_element_type=F32)
 
     def gy_copy(rel):
-        return remote(gmy.at[0], gmy.at[rel], gy_ss.at[rel], gy_rs.at[rel], at_y(rel))
+        return remote(gmy.at[0], gmy.at[rel], gm_ss.at[0], gm_rs.at[0], at_y(rel))
+
+    def gy_all():
+        return remote(gmy.at[pl.ds(0, 3)], gmy.at[pl.ds(0, 3)], gm_ss.at[0], gm_rs.at[0], at_y(1))
 
     def gx_copy(d):
-        return remote(gma.at[0], gma.at[d], gx_ss.at[d], gx_rs.at[d], at_x(d))
+        return remote(gma.at[0], gma.at[d], gm_ss.at[1], gm_rs.at[1], at_x(d))
+
+    def gx_all():
+        return remote(gma.at[others], gma.at[others], gm_ss.at[1], gm_rs.at[1], at_x(1))
 
     def ta_copy():
         return remote(gma.at[16], gma.at[17], ta_sem.at[0], ta_sem.at[1], twin)
@@ -538,15 +566,14 @@
 
     def sums(t, meanwhile):
         for c in range(2):
-            for i in (2, 3, 4, 5):
-                rs_copy(t, c, i).wait_recv()
+            rs_rest(t, c)
             sum_and_send(t, c)
         meanwhile()
-        over_gx(lambda d: hb_copy(t, 0, d).wait_recv())
-        over_gx(lambda d: hb_copy(t, 1, d).wait_recv())
+        arrived(HB, t, 0)
+        arrived(HB, t, 1)
         x_third(t)
-        over_gx(lambda d: h_copy(t, 0, d).wait_recv())
-        over_gx(lambda d: h_copy(t, 1, d).wait_recv())
+        arrived(H, t, 0)
+        arrived(H, t, 1)
 
     sums(0, lambda: None)
 
@@ -566,16 +593,10 @@
         ag_forward(t, 1)
 
     gather(0, u)
-    for i in range(6):
-        rs_copy(0, 0, i).wait_send()
-        rs_copy(0, 1, i).wait_send()
-    for xc in range(2):
-        over_gx(lambda d: h_copy(0, xc, d).wait_send())
-        over_gx(lambda d: b_copy(0, xc, d).wait_send())
-        over_gx(lambda d: hb_copy(0, xc, d).wait_send())
-        over_gx(lambda d: bb_copy(0, xc, d).wait_send())
-    for rel in (1, 2, 3):
-        pb_copy(0, rel).wait_send()
+    rs_sent(0)
+    for kind in (H, B, HB, BB):
+        departed(kind, 0)
+    pb_all(0).wait_send()
 
     ag_finish(0, 0)
     gather_third(0, 0)
@@ -616,13 +637,12 @@
     lax.fori_loop(0, 3, adjoint_block, 0, unroll=True)
     x_inverse_and_send(1)
     weight_gradient_send()
-    for rel in (1, 2, 3):
-        gy_copy(rel).wait_recv()
+    gy_all().wait_recv()
     gma[0] = gmy[0] + gmy[1] + gmy[2] + gmy[3]
     over_gx(lambda d: gx_copy(d).start())
     build_kron(TN)
     gather(1, g)
-    over_gx(lambda d: gx_copy(d).wait_recv())
+    gx_all().wait_recv()
     gma[16] = jnp.sum(gma[0:16], 0)
     ta_copy().start()
     weight_gradient_finish()
@@ -647,24 +667,17 @@
     for cb in range(5):
         gm_ref[cb * 4:(cb + 1) * 4, :] = total[cb * 8:cb * 8 + 4, :C]
 
-    for i in range(6):
-        for c in range(2):
-            ag_copy(0, c, i).wait_send()
-            ag_copy(1, c, i).wait_send()
-            rs_copy(1, c, i).wait_send()
-    for xc in range(2):
-        over_gx(lambda d: h_copy(1, xc, d).wait_send())
-        over_gx(lambda d: b_copy(1, xc, d).wait_send())
-        over_gx(lambda d: hb_copy(1, xc, d).wait_send())
-        over_gx(lambda d: bb_copy(1, xc, d).wait_send())
-    for rel in (1, 2, 3):
-        pb_copy(1, rel).wait_send()
-        yb_copy(0, rel).wait_send()
-        yb_copy(1, rel).wait_send()
+    ag_sent(0)
+    ag_sent(1)
+    rs_sent(1)
+    for kind in (H, B, HB, BB):
+        departed(kind, 1)
+    pb_all(1).wait_send()
+    yb_all(0).wait_send()
+    yb_all(1).wait_send()
     gs_copy().wait_send()
-    for rel in (1, 2, 3):
-        gy_copy(rel).wait_send()
-    over_gx(lambda d: gx_copy(d).wait_send())
+    gy_all().wait_send()
+    gx_all().wait_send()
     ta_copy().wait_send()
     gf_out[0].wait()
     gf_out[1].wait()
@@ -756,27 +769,17 @@
             vmem((18, 40, 128), F32),
             dma((16,)),
             dma((2, 2)),
-            dma((2, 2, 6)),
-            dma((2, 2, 6)),
-            dma((2, 2, GX)),
-            dma((2, 2, GX)),
-            dma((2, 2, GX)),
-            dma((2, 2, GX)),
-            dma((2, 2, 6)),
-            dma((2, 2, 6)),
-            dma((2, 2, GX)),
-            dma((2, 2, GX)),
-            dma((2, 2, GX)),
-            dma((2, 2, GX)),
-            dma((2, GY)),
-            dma((2, GY)),
-            dma((2, GY)),
-            dma((2, GY)),
             dma((2,)),
-            dma((4,)),
-            dma((4,)),
-            dma((GX,)),
-            dma((GX,)),
+            dma((2, 2, 3)),
+            dma((2,)),
+            dma((2, 2, 3)),
+            dma((4, 2)),
+            dma((4, 2, 2)),
+            dma((2, 2)),
+            dma((2, 2)),
+            dma((2,)),
+            dma((2,)),
+            dma((2,)),
             dma((2,)),
         ],
         compiler_params=pltpu.CompilerParams(

time: 111 us -> 104 us (0.937)
  Pallas kernels: 110 us -> 103 us
    pallas_call x1, Pallas kernels: 104 us -> 97.1 us  [shards(): pl.pallas_call(kernel, out_shape=results, in_specs=[hbm, hbm, hbm, local]...]
where the time goes in v4:
time: 104 us
  Pallas kernels  103 us (99%)
    pallas_call x1, Pallas kernels, shards(): pl.pallas_call(kernel, out_shape=results, in_specs=[hbm, hbm, hbm, local]...  97.1 us
    pallas_call x1, Pallas kernels, shards(): pl.pallas_call(hand_over, out_shape=results, in_specs=[hbm] * 4, out_spec...  5.69 us

profile of v4, /device:TPU:0, one launch (start us, length us, event | category | flops | bytes accessed | tf_op | source)
XLA Modules:
  0.0 103.6 jit_solution(7135810875741996397)
XLA Ops:
  0.6 97.1 %shard_map.156 = (bf16[1024,1280]{1,0:T(8,128)(2,1)}, bf16[1024,1280]{1,0:T(8,128)(2,1)}, f32[3,3,20,2,960]{4,3,2,1,0:T(2,128)}, f32[20,20]{1,0:T(8,128)}) custom-call(bf16[1024,1280]{1,0:T(8,128)(2,1)} %bitcast.6, bf16[1024,1280]{1,0:T(8,128)(2,1)} %bitcast.7, bf16[3,6,20,2,960]{4,3,2,1,0:T(2,128)(2,1)} %bitcast.8, bf16[20,20]{1,0:T(8,128)(2,1)} %mix_ref.1, ...), custom_call_target="tpu_custom_call" | custom-call | tf_op jit(solution)/shard_map/pallas_call | solution.py:715
  97.7 5.7 %shard_map.157 = (bf16[1024,1280]{1,0:T(8,128)(2,1)}, bf16[1024,1280]{1,0:T(8,128)(2,1)}, f32[3,3,20,2,960]{4,3,2,1,0:T(2,128)}, f32[20,20]{1,0:T(8,128)}) custom-call(bf16[1024,1280]{1,0:T(8,128)(2,1)} %get-tuple-element.12.act_in, bf16[1024,1280]{1,0:T(8,128)(2,1)} %get-tuple-element.13.gf_in, f32[3,3,20,2,960]{4,3,2,1,0:T(2,128)} %get-tuple-element.14.gs_in, ...), custom_call_target="tpu_custom_call" | custom-call | tf_op jit(solution)/shard_map/pallas_call | solution.py:792

commit v5 on v4

--- a/solution.py
+++ b/solution.py
@@ -227,16 +227,18 @@
         tab = [ee[lax.rem(me_y + rel, GY)] for rel in rels]
         tab = tab[0] if len(tab) == 1 else jnp.concatenate(tab, 1)
         both = jnp.dot(src[xc * HALF:(xc + 1) * HALF, :], tab, preferred_element_type=F32).astype(BF16)
-        for i, rel in enumerate(rels):
-            d = both[:, i * 256:(i + 1) * 256]
-            for xp in range(4):
-                r = xp * 128
-                rhs = jnp.concatenate(
-                    [d[r:r + 64, :128], d[r:r + 64, 128:], d[r + 64:r + 128, :128], d[r + 64:r + 128, 128:]], 0
+        for xp in range(4):
+            r = xp * 128
+            rhs = jnp.concatenate([
+                jnp.concatenate(
+                    [both[row:row + 64, i * 256 + p * 128:i * 256 + p * 128 + 128] for i in range(len(rels))], 1
                 )
-                o = jnp.dot(a2[...], rhs, preferred_element_type=F32)
-                part[rel, xc, xp * 128:(xp + 1) * 128, :] = o[:128].astype(BF16)
-                sb[i, xp * 64:(xp + 1) * 64, :] = o[128:]
+                for row in (r, r + 64) for p in range(2)
+            ], 0)
+            o = jnp.dot(a2[...], rhs, preferred_element_type=F32)
+            for i, rel in enumerate(rels):
+                part[rel, xc, xp * 128:(xp + 1) * 128, :] = o[:128, i * 128:(i + 1) * 128].astype(BF16)
+                sb[i, xp * 64:(xp + 1) * 64, :] = o[128:, i * 128:(i + 1) * 128]
         for i, rel in enumerate(rels):
             for gx in range(GX):
                 top = sb[i, pl.ds(gx, 8, stride=32), :]
@@ -357,29 +359,28 @@
             agb[rel] = sb[rel].astype(BF16)
 
     def y_inverse(t, xc):
-        for rel in range(GY):
-            h = lax.rem(me_y + rel, GY)
-            off = pl.multiple_of(h * 256, 256)
-            for xp in range(4):
-                rhs = jnp.concatenate(
-                    [ag[t, rel, xc, xp * 128:(xp + 1) * 128, :], agb[rel, xp * 64:(xp + 1) * 64, :]], 0
-                )
-                v = jnp.dot(at2[...], rhs, preferred_element_type=F32).astype(BF16)
+        for xp in range(4):
+            two, third = slice(xp * 128, (xp + 1) * 128), slice(xp * 64, (xp + 1) * 64)
+            rhs = jnp.concatenate([
+                jnp.concatenate([ag[t, rel, xc, two, :] for rel in range(GY)], 1),
+                jnp.concatenate([agb[rel, third, :] for rel in range(GY)], 1),
+            ], 0)
+            v = jnp.dot(at2[...], rhs, preferred_element_type=F32).astype(BF16)
+            for rel in range(GY):
+                off = pl.multiple_of(lax.rem(me_y + rel, GY) * 256, 256)
+                w_rel = v[:, rel * 128:(rel + 1) * 128]
                 for x2 in range(2):
                     rows = slice(xp * 128 + x2 * 64, xp * 128 + x2 * 64 + 64)
-                    by[rows, pl.ds(off, 128)] = v[x2 * 128:x2 * 128 + 64]
-                    by[rows, pl.ds(off + 128, 128)] = v[x2 * 128 + 64:x2 * 128 + 128]
-
-    def depth_inverse(xc, finish, start=0, stop=5):
-        def block(n, carry):
-            cols = pl.ds(pl.multiple_of(n * 256, 256), 256)
+                    by[rows, pl.ds(off, 128)] = w_rel[x2 * 128:x2 * 128 + 64]
+                    by[rows, pl.ds(off + 128, 128)] = w_rel[x2 * 128 + 64:x2 * 128 + 128]
+
+    def depth_inverse(xc, finish, start=0, stop=3):
+        for n in range(start, stop):
+            cols = slice(n * 512, min(n * 512 + 512, CZ))
             for rb in range(2):
                 rows = slice(xc * HALF + rb * 256, xc * HALF + rb * 256 + 256)
                 v = jnp.dot(by[rb * 256:rb * 256 + 256, :], eet[:, cols], preferred_element_type=F32)
                 finish(rows, cols, v + lin[rows, cols])
-            return carry
-
-        lax.fori_loop(start, stop, block, 0, unroll=True)
 
     def finish_forward(rows, cols, x):
         k0 = math.sqrt(2.0 / math.pi)
@@ -568,10 +569,10 @@
         for c in range(2):
             rs_rest(t, c)
             sum_and_send(t, c)
-        meanwhile()
         arrived(HB, t, 0)
         arrived(HB, t, 1)
         x_third(t)
+        meanwhile()
         arrived(H, t, 0)
         arrived(H, t, 1)
 
@@ -615,9 +616,9 @@
     ag_finish(0, 1)
     gather_third(0, 1)
     y_inverse(0, 1)
-    depth_inverse(1, finish_forward, 0, 3)
+    depth_inverse(1, finish_forward, 0, 2)
     rs_forward(1, 0)
-    depth_inverse(1, finish_forward, 3, 5)
+    depth_inverse(1, finish_forward, 2, 3)
     act_out[1].start()
     forward_block(g, 1, 2, 1)
     rs_start(1, 1, 0, 1, 2)

time: 104 us -> 99.2 us (0.954)
  Pallas kernels: 103 us -> 98.2 us
    pallas_call x1, Pallas kernels: 97.1 us -> 92.5 us  [shards(): pl.pallas_call(kernel, out_shape=results, in_specs=[hbm, hbm, hbm, local]...]
where the time goes in v5:
time: 99.2 us; the launch traced here: 99 us
  Pallas kernels  98.2 us (99%)
    pallas_call x1, Pallas kernels, shards(): pl.pallas_call(kernel, out_shape=results, in_specs=[hbm, hbm, hbm, local]...  92.5 us
    pallas_call x1, Pallas kernels, shards(): pl.pallas_call(hand_over, out_shape=results, in_specs=[hbm] * 4, out_spec...  5.69 us

profile of v5, /device:TPU:0, one launch (start us, length us, event | category | flops | bytes accessed | tf_op | source)
XLA Modules:
  0.0 99.0 jit_solution(16319189047167228681)
XLA Ops:
  0.6 92.5 %shard_map.156 = (bf16[1024,1280]{1,0:T(8,128)(2,1)}, bf16[1024,1280]{1,0:T(8,128)(2,1)}, f32[3,3,20,2,960]{4,3,2,1,0:T(2,128)}, f32[20,20]{1,0:T(8,128)}) custom-call(bf16[1024,1280]{1,0:T(8,128)(2,1)} %bitcast.6, bf16[1024,1280]{1,0:T(8,128)(2,1)} %bitcast.7, bf16[3,6,20,2,960]{4,3,2,1,0:T(2,128)(2,1)} %bitcast.8, bf16[20,20]{1,0:T(8,128)(2,1)} %mix_ref.1, ...), custom_call_target="tpu_custom_call" | custom-call | tf_op jit(solution)/shard_map/pallas_call | solution.py:716
  93.1 5.7 %shard_map.157 = (bf16[1024,1280]{1,0:T(8,128)(2,1)}, bf16[1024,1280]{1,0:T(8,128)(2,1)}, f32[3,3,20,2,960]{4,3,2,1,0:T(2,128)}, f32[20,20]{1,0:T(8,128)}) custom-call(bf16[1024,1280]{1,0:T(8,128)(2,1)} %get-tuple-element.12.act_in, bf16[1024,1280]{1,0:T(8,128)(2,1)} %get-tuple-element.13.gf_in, f32[3,3,20,2,960]{4,3,2,1,0:T(2,128)} %get-tuple-element.14.gs_in, ...), custom_call_target="tpu_custom_call" | custom-call | tf_op jit(solution)/shard_map/pallas_call | solution.py:793

commit v6 on v5

--- a/solution.py
+++ b/solution.py
@@ -599,8 +599,8 @@
         departed(kind, 0)
     pb_all(0).wait_send()
 
+    gather_third(0, 0)
     ag_finish(0, 0)
-    gather_third(0, 0)
     y_inverse(0, 0)
     depth_inverse(0, finish_forward)
     act_out = [
@@ -613,8 +613,8 @@
     forward_block(g, 0, 3, 0)
     rs_start(1, 0, 3)
     send_third(1, 0)
+    gather_third(0, 1)
     ag_finish(0, 1)
-    gather_third(0, 1)
     y_inverse(0, 1)
     depth_inverse(1, finish_forward, 0, 2)
     rs_forward(1, 0)
@@ -649,8 +649,8 @@
     weight_gradient_finish()
     act_out[0].wait()
     act_out[1].wait()
+    gather_third(1, 0)
     ag_finish(1, 0)
-    gather_third(1, 0)
     y_inverse(1, 0)
     depth_inverse(0, finish_backward)
     gf_out = [
@@ -658,8 +658,8 @@
         for xc in range(2)
     ]
     gf_out[0].start()
+    gather_third(1, 1)
     ag_finish(1, 1)
-    gather_third(1, 1)
     y_inverse(1, 1)
     depth_inverse(1, finish_backward)
     gf_out[1].start()

time: 99.2 us -> 99.4 us (level)
  no operation moved by 1% of the time
where the time goes in v6:
time: 99.4 us; the launch traced here: 99.2 us
  Pallas kernels  98.4 us (99%)
    pallas_call x1, Pallas kernels, shards(): pl.pallas_call(kernel, out_shape=results, in_specs=[hbm, hbm, hbm, local]...  92.7 us
    pallas_call x1, Pallas kernels, shards(): pl.pallas_call(hand_over, out_shape=results, in_specs=[hbm] * 4, out_spec...  5.69 us

profile of v6, /device:TPU:0, one launch (start us, length us, event | category | flops | bytes accessed | tf_op | source)
XLA Modules:
  0.0 99.2 jit_solution(12389638658524997675)
XLA Ops:
  0.6 92.7 %shard_map.156 = (bf16[1024,1280]{1,0:T(8,128)(2,1)}, bf16[1024,1280]{1,0:T(8,128)(2,1)}, f32[3,3,20,2,960]{4,3,2,1,0:T(2,128)}, f32[20,20]{1,0:T(8,128)}) custom-call(bf16[1024,1280]{1,0:T(8,128)(2,1)} %bitcast.6, bf16[1024,1280]{1,0:T(8,128)(2,1)} %bitcast.7, bf16[3,6,20,2,960]{4,3,2,1,0:T(2,128)(2,1)} %bitcast.8, bf16[20,20]{1,0:T(8,128)(2,1)} %mix_ref.1, ...), custom_call_target="tpu_custom_call" | custom-call | tf_op jit(solution)/shard_map/pallas_call | solution.py:716
  93.3 5.7 %shard_map.157 = (bf16[1024,1280]{1,0:T(8,128)(2,1)}, bf16[1024,1280]{1,0:T(8,128)(2,1)}, f32[3,3,20,2,960]{4,3,2,1,0:T(2,128)}, f32[20,20]{1,0:T(8,128)}) custom-call(bf16[1024,1280]{1,0:T(8,128)(2,1)} %get-tuple-element.12.act_in, bf16[1024,1280]{1,0:T(8,128)(2,1)} %get-tuple-element.13.gf_in, f32[3,3,20,2,960]{4,3,2,1,0:T(2,128)} %get-tuple-element.14.gs_in, ...), custom_call_target="tpu_custom_call" | custom-call | tf_op jit(solution)/shard_map/pallas_call | solution.py:793
